TPU v7x, 512 devices: a whole 4x4x16 slice. The times are simulated.
512 devices in a mesh: feat: 64 (over z, y), tok: 8 (over x, core).
Axes of the slice: x: 4, y: 4, z: 16, core: 2. Of those that a mesh axis runs over, the one named last changes fastest.
Arguments:
- acts: bfloat16 [4096, 2048], P('feat', 'tok')
- dec_bias: float32 [4096], P('feat'), may hold values from -3 to 3
- enc_weight: bfloat16 [4096, 16384], P(None, 'feat')
- enc_bias: float32 [16384], P('feat'), may hold values from -3 to 3
- dec_weight: bfloat16 [16384, 4096], P('feat'), may hold values from -0.046875 to 0.046875
- dead_ids: int32 [64, 256], P('feat'), may hold values from 0 to 255, each once within a row
- tile_count: int32 [64, 8], replicated, may hold values from 0 to 32, as said below
- sample_rows: int32 [64, 8, 32], P(None, 'tok'), may hold values from 0 to 255
Outputs:
- new_enc: bfloat16 [16384, 4096], P(('feat', 'tok'))
- new_dec: bfloat16 [16384, 4096], P(('feat', 'tok'))
- reencoded: bfloat16 [2048, 16384], P('tok', 'feat')
- token_loss: float32 [2048], P('tok')
Inputs may be any that keep to these rules, and one draw needn't show every extreme that they name: `tile_count`: in every shard some tile holds fewer than 32 valid slots, and some tile of some shard is full. Each row of dead_ids names every latent of its shard once.
All inputs are finite; a program needn't handle non-finite values.
Results may differ from a plain program's by a relative error of at most 0.0062.
Values may be sent and summed in bfloat16 or wider, within the bound.
No kernel may reach another device: no remote copies, remote signals or barrier semaphores. Data moves between devices by JAX's collectives and lax.ppermute only.
A program may use at most 64 MiB of HBM per device.

v0:
```python
import jax
import jax.numpy as jnp
from jax import lax
from jax.sharding import PartitionSpec as P

ENC_GAIN = 0.2
EPSILON = 1e-06


def on_device(acts, dec_bias, enc_weight, enc_bias, dec_weight, dead_ids, tile_count, sample_rows):
    n_feat = lax.axis_size("feat")
    n_tok = lax.axis_size("tok")
    feat_index = lax.axis_index("feat")
    tok_index = lax.axis_index("tok")
    width = enc_weight.shape[0]
    latents = enc_weight.shape[1]
    tokens_dev = acts.shape[1]
    tile = sample_rows.shape[2]
    slots = dead_ids.shape[1]
    centered_local = (acts.astype(jnp.float32) - dec_bias[:, None]).astype(jnp.bfloat16)
    my_counts = lax.dynamic_index_in_dim(tile_count, feat_index, 0, keepdims=False)
    slot_numbers = jnp.arange(slots, dtype=jnp.int32)
    slot_tile = slot_numbers // tile
    slot_place = slot_numbers % tile
    tile_numbers = jnp.arange(n_tok, dtype=jnp.int32)
    matches = (slot_tile[:, None] == tile_numbers[None, :]) & (
        slot_place[:, None] < my_counts[None, :]
    )
    valid_slots = jnp.any(matches, axis=1)
    latent_numbers = jnp.arange(latents, dtype=jnp.int32)
    hits = (dead_ids[0][:, None] == latent_numbers[None, :]) & valid_slots[:, None]
    alive = 1.0 - jnp.any(hits, axis=0).astype(jnp.float32)
    col_norms = jnp.sqrt(
        jnp.einsum("dj,dj->j", enc_weight, enc_weight, preferred_element_type=jnp.float32)
    )
    stat_local = jnp.sum(col_norms * alive)
    alive_total = (n_feat * latents - jnp.sum(tile_count)).astype(jnp.float32)
    stat_sum = lax.psum(stat_local, "feat")
    piece = lax.all_gather(centered_local, "feat", axis=0, tiled=True)
    preact = lax.dot_general(
        piece, enc_weight, (((0,), (0,)), ((), ())), preferred_element_type=jnp.float32
    )
    preact, centered = (preact, piece)
    features = (jnp.maximum(preact + enc_bias, 0.0) * alive).astype(jnp.bfloat16)
    rows_dev = tokens_dev // n_feat
    recon = lax.psum_scatter(
        jnp.dot(features, dec_weight, preferred_element_type=jnp.float32),
        "feat",
        scatter_dimension=0,
        tiled=True,
    )
    own_tokens = lax.dynamic_slice_in_dim(centered, feat_index * rows_dev, rows_dev, 1)
    error = own_tokens.T.astype(jnp.float32) - recon
    loss_part = lax.dynamic_update_slice_in_dim(
        jnp.zeros((tokens_dev,), jnp.float32),
        jnp.sum(error * error, axis=1),
        feat_index * rows_dev,
        0,
    )
    error_all = lax.all_gather(error.astype(jnp.bfloat16), "feat", axis=0, tiled=True)
    own_samples = lax.dynamic_index_in_dim(sample_rows[:, 0, :], feat_index, 0, keepdims=False)
    tile_rows = jnp.take(error_all, own_samples, axis=0)
    loss_sum = lax.psum(loss_part, "feat")
    token_loss = loss_sum / width
    mean_norm = stat_sum / alive_total
    my_count = lax.dynamic_index_in_dim(my_counts, tok_index, 0, keepdims=False)
    tile_valid = (jnp.arange(tile, dtype=jnp.int32) < my_count).astype(jnp.float32)
    rows_f = tile_rows.astype(jnp.float32)
    scale = lax.rsqrt(jnp.sum(rows_f * rows_f, axis=1, keepdims=True) + EPSILON)
    unit = rows_f * scale * tile_valid[:, None]
    new_dec = unit.astype(jnp.bfloat16)
    new_enc = (ENC_GAIN * mean_norm * unit).astype(jnp.bfloat16)
    product = lax.dot_general(
        centered,
        lax.all_gather(new_enc, "tok", axis=0, tiled=True),
        (((0,), (1,)), ((), ())),
        preferred_element_type=jnp.float32,
    )
    reencoded = jnp.maximum(product, 0.0).astype(jnp.bfloat16)
    return (new_enc, new_dec, reencoded, token_loss)


def solution(mesh):
    in_specs = (
        P("feat", "tok"),
        P("feat"),
        P(None, "feat"),
        P("feat"),
        P("feat", None),
        P("feat", None),
        P(),
        P(None, "tok", None),
    )
    out_specs = (P(("feat", "tok"), None), P(("feat", "tok"), None), P("tok", "feat"), P("tok"))
    return jax.shard_map(
        on_device, mesh=mesh, in_specs=in_specs, out_specs=out_specs, check_vma=False
    )
```

profile of v0, /device:TPU:1, one launch (start us, length us, event | category | flops | bytes accessed | tf_op | source)
XLA Modules:
  0.0 647.6 jit_solution(14248546136938520552)
XLA Ops:
  7.2 0.0 copy-start
  7.2 0.0 copy-start.3
  7.2 0.0 all-gather.5.cloned.1.call-start
  7.2 1.6 subtract_convert_fusion
  8.8 0.0 all-gather.5.cloned.1.call-update
  8.9 0.0 all-reduce.4.cloned.1.call-start
  8.9 0.9 dynamic-slice_reduce_fusion.1
  9.8 0.1 fusion.19
  9.9 0.8 fusion.14
  10.7 2.2 fusion
  12.9 0.6 multiply_reduce_fusion.1
  13.5 135.5 %all-gather.5.cloned.1.call-done = bf16[4096,256]{1,0:T(8,128)(2,1)} async-done(((bf16[64,256]{1,0:T(8,128)(2,1)}), bf16[4096,256]{1,0:T(8,128)(2,1)}) %all-gather.5.cloned.1.call-update) | async-done | bytes 2097168 | tf_op jit(solution)/shard_map/all_gather | solution.py:39
  149.0 0.0 copy-done
  149.0 0.0 copy-done.3
  149.0 6.6 %fusion.6 = f32[256,4096]{1,0:T(8,128)} fusion(bf16[256,4096]{1,0:T(8,128)(2,1)S(1)} %copy-done, bf16[4096,256]{1,0:T(8,128)(2,1)} %all-gather.5.cloned.1.call-done, bf16[4096,256]{1,0:T(8,128)(2,1)} %param.10, f32[256]{0:T(256)S(1)} %get-tuple-element.11, f32[256]{0:T(256)S(1)} %copy-done.3), kind=kOutput, calls=%fused_computation.12 | convolution fusion | flops 1074003968 | bytes 10487808 | tf_op jit(solution)/shard_map/dot_general | solution.py:47
  155.6 0.0 all-reduce.4.cloned.1.call-update
  155.6 0.0 all-gather.9.cloned.1.call-start
  155.7 1.3 dynamic-slice.2
  157.6 283.6 %all-reduce.4.cloned.1.call-done = f32[256,4096]{1,0:T(8,128)} async-done(((f32[256,4096]{1,0:T(8,128)}), f32[256,4096]{1,0:T(8,128)}) %all-reduce.4.cloned.1.call-update) | async-done | bytes 4194320
  441.2 0.9 constant_dynamic-slice_fusion
  442.1 2.0 copy.16
  444.1 0.0 copy-start.1
  444.1 0.0 copy-start.2
  444.1 2.5 multiply_reduce_fusion
  446.7 1.0 copy.17
  447.7 0.0 all-gather.9.cloned.1.call-update
  447.7 0.0 all-gather.7.cloned.1.call-start
  447.7 0.0 copy-done.1
  447.7 0.6 reduce_sum.37
  449.0 0.6 dynamic_slice.18
  449.6 0.0 copy-done.2
  449.6 0.2 dynamic-slice_reduce_fusion
  449.8 0.7 compare_convert_fusion
  450.5 0.2 dynamic_update_slice.3
  450.7 114.7 %all-reduce.1 = (f32[]{:T(128)}, f32[256]{0:T(256)S(1)}) all-reduce(f32[]{:T(128)} %get-tuple-element.10, f32[256]{0:T(256)S(1)} %dynamic_update_slice.3), channel_id=1, replica_groups=mesh['feat'=64,'tok'=8] {'feat'}, use_global_device_ids=true, to_apply=%region_3.4 | all-reduce | flops 257 | bytes 2056 | tf_op jit(solution)/shard_map/psum | solution.py:38
  566.1 17.7 %all-gather.9.cloned.1.call-done = bf16[64,4,4096]{2,1,0:T(4,128)(2,1)} async-done(((bf16[1,4,4096]{2,1,0:T(4,128)(2,1)}), bf16[64,4,4096]{2,1,0:T(4,128)(2,1)}) %all-gather.9.cloned.1.call-update) | async-done | bytes 2097168 | tf_op jit(solution)/shard_map/all_gather | solution.py:60
  583.8 4.0 reshape.96
  587.7 2.8 gather_fusion
  590.5 0.3 fusion.8
  590.8 1.0 fusion.10
  591.8 0.0 all-gather.7.cloned.1.call-update
  591.8 0.6 broadcast_multiply_fusion
  592.4 45.1 %all-gather.7.cloned.1.call-done = bf16[256,4096]{1,0:T(8,128)(2,1)} async-done(((bf16[32,4096]{1,0:T(8,128)(2,1)}), bf16[256,4096]{1,0:T(8,128)(2,1)}) %all-gather.7.cloned.1.call-update) | async-done | bytes 2097168 | tf_op jit(solution)/shard_map/all_gather | solution.py:75
  637.4 3.6 fusion.5
  (5 shorter events, 0.0 us)
Async XLA Ops:
  7.2 141.8 %copy-start = (bf16[256,4096]{1,0:T(8,128)(2,1)S(1)}, bf16[256,4096]{1,0:T(8,128)(2,1)}, u32[]{:S(2)}) copy-start(bf16[256,4096]{1,0:T(8,128)(2,1)} %param.12) | copy-start | bytes 6291460
  7.2 141.8 %copy-start.3 = (f32[256]{0:T(256)S(1)}, f32[256]{0:T(256)}, u32[]{:S(2)}) copy-start(f32[256]{0:T(256)} %param.11) | copy-start | bytes 3076
  7.2 141.8 %all-gather.5.cloned.1.call-start = ((), (), s32[]{:S(2)}) async-start(), calls=%async_computation | async-start | bytes 2129920 | tf_op jit(solution)/shard_map/all_gather | solution.py:39
  8.9 432.4 %all-reduce.4.cloned.1.call-start = ((), (), s32[]{:S(2)}) async-start(), calls=%async_computation.3 | async-start | bytes 8388608
  155.6 428.1 %all-gather.9.cloned.1.call-start = ((), (), s32[]{:S(2)}) async-start(), calls=%async_computation.2 | async-start | bytes 2129920 | tf_op jit(solution)/shard_map/all_gather | solution.py:60
  444.1 3.6 copy-start.1
  444.1 5.5 copy-start.2
  447.7 189.8 %all-gather.7.cloned.1.call-start = ((), (), s32[]{:S(2)}) async-start(), calls=%async_computation.1 | async-start | bytes 2359296 | tf_op jit(solution)/shard_map/all_gather | solution.py:75
Sparse Core Ops, SparseCore 0:
  11.5 137.4 all-gather.4
  155.8 285.4 all-reduce.3
  447.8 135.9 all-gather.8
  591.9 45.4 all-gather.6
where the time goes:
time: 648 us
  waiting for transfers between devices  482 us (74%)
  blocking collectives  115 us (18%)
  between operations  15.8 us (2%)
  local copies, waits for them, and re-layouts  13.9 us (2%)
  other arithmetic  10.9 us (2%)
  matrix products  10.2 us (2%)
    unnamed x5, waiting for transfers between devices  284 us
    all_gather x1, waiting for transfers between devices, on_device(): piece = lax.all_gather(centered_local, 'feat', axis=0, tiled=True)  136 us
    psum x1, blocking collectives, on_device(): stat_sum = lax.psum(stat_local, 'feat')  115 us
    all_gather x1, waiting for transfers between devices, on_device(): lax.all_gather(new_enc, 'tok', axis=0, tiled=True)  45.1 us
    all_gather x1, waiting for transfers between devices, on_device(): lax.all_gather(error.astype(jnp.bfloat16), 'feat', axis=0, tiled=True)  17.7 us
  transfers between devices with their start and end apart: 4, of which 4 were waited for; matrix products, arithmetic and copies ran while one was open for 1% of the time, Pallas kernels for 0%

commit v1 on v0

v1 whole, which is shorter than its diff:
```python
import jax
import jax.numpy as jnp
from jax import lax
from jax.experimental import pallas as pl
from jax.experimental.pallas import tpu as pltpu
from jax.sharding import Mesh, PartitionSpec as P

ENC_GAIN = 0.2
EPSILON = 1e-06
F32 = jnp.float32
BF16 = jnp.bfloat16
VM = pl.BlockSpec(memory_space=pltpu.VMEM)
SM = pl.BlockSpec(memory_space=pltpu.SMEM)
EXTRA = 16


def kernel_call(body, out_shape, in_specs, flops, nbytes, scratch=()):
    multi = isinstance(out_shape, (tuple, list))
    return pl.pallas_call(
        body,
        out_shape=out_shape,
        in_specs=in_specs,
        out_specs=[VM] * len(out_shape) if multi else VM,
        scratch_shapes=list(scratch),
        compiler_params=pltpu.CompilerParams(vmem_limit_bytes=24 << 20),
        cost_estimate=pl.CostEstimate(flops=flops, bytes_accessed=nbytes, transcendentals=0),
    )


def split3(v):
    hi = v.astype(BF16)
    rest = v - hi.astype(F32)
    mid = rest.astype(BF16)
    lo = (rest - mid.astype(F32)).astype(BF16)
    return hi, mid, lo


def prepare(enc_ref, dec_ref, alive_ref, rows_ref, enc_t_ref, dec_t_ref, onehot_ref, stat_ref):
    latents = enc_ref.shape[1]
    total = jnp.zeros((1, latents), F32)
    for y in range(4):
        for pair in range(8):
            parts = []
            for z in (2 * pair, 2 * pair + 1):
                block = enc_ref[pl.ds((z * 4 + y) * 64, 64), :]
                wide = block.astype(F32)
                total = total + jnp.sum(wide * wide, axis=0, keepdims=True)
                parts.append(block)
            enc_t_ref[:, pl.ds(y * 1024 + pair * 128, 128)] = jnp.concatenate(parts, 0).T
    stat_ref[...] = jnp.sum(jnp.sqrt(total) * alive_ref[...], axis=1, keepdims=True)
    for block in range(16):
        dec_t_ref[pl.ds(block * 256, 256), :] = dec_ref[:, pl.ds(block * 256, 256)].T
    tokens = onehot_ref.shape[0]
    for block in range(16):
        cols = pl.ds(block * 128, 128)
        token = lax.broadcasted_iota(jnp.int32, (tokens, 128), 0)
        onehot_ref[:, cols] = jnp.where(token == rows_ref[:, cols], 1.0, 0.0).astype(BF16)


def turn(g_ref, out_ref):
    for z in range(16):
        for pair in range(2):
            y = 2 * pair
            both = jnp.concatenate(
                [
                    g_ref[pl.ds((y * 16 + z) * 64, 64), :],
                    g_ref[pl.ds(((y + 1) * 16 + z) * 64, 64), :],
                ],
                0,
            )
            out_ref[:, pl.ds(z * 256 + pair * 128, 128)] = both.T


def forward(enc_t_ref, g_ref, bias_ref, alive_ref, dec_t_ref, out_ref):
    pre = jnp.dot(enc_t_ref[...], g_ref[...], preferred_element_type=F32)
    feat = (jnp.maximum(pre + bias_ref[...], 0.0) * alive_ref[...]).astype(BF16)
    for block in range(16):
        rows = pl.ds(block * 256, 256)
        out_ref[rows, :] = jnp.dot(
            dec_t_ref[rows, :], feat, preferred_element_type=F32
        ).astype(BF16)


def residual(part_ref, own_ref, onehot_ref, stat_ref, out_ref):
    recon = part_ref[0].astype(F32)
    for z in range(1, 16):
        recon = recon + part_ref[z].astype(F32)
    error = own_ref[...].astype(F32) - recon
    loss = jnp.sum(error * error, axis=0, keepdims=True)
    loss = jnp.concatenate([loss[:, :128], loss[:, 128:]], 0)
    stat = jnp.broadcast_to(stat_ref[...], (2, 128))
    pad = jnp.zeros((4, 128), F32)
    pieces = [split3(v) for v in (loss, stat)]
    extra = jnp.concatenate([p.astype(F32) for s in pieces for p in s] + [pad], 0).astype(BF16)
    error_b = error.astype(BF16)
    for z in range(16):
        picked = jnp.dot(
            error_b, onehot_ref[:, pl.ds(z * 128, 128)], preferred_element_type=F32
        )
        out_ref[z, pl.ds(0, 64), :] = picked.astype(BF16)
        out_ref[z, pl.ds(64, EXTRA), :] = extra


def relay(in_ref, out_ref):
    riders = in_ref[0, pl.ds(64, EXTRA), :].astype(F32)
    hi, mid, lo = riders[0:2], riders[2:4], riders[4:6]
    shi, smid, slo = riders[6:8], riders[8:10], riders[10:12]
    loss = hi + mid + lo
    stat = shi + smid + slo
    for z in range(1, 16):
        riders = in_ref[z, pl.ds(64, EXTRA), :].astype(F32)
        loss = loss + (riders[0:2] + riders[2:4] + riders[4:6])
        stat = stat + (riders[6:8] + riders[8:10] + riders[10:12])
    row = jnp.concatenate([loss[0:1], loss[1:2], stat[0:1]], 1)
    row = jnp.concatenate(
        [p.astype(F32) for p in split3(row)] + [jnp.zeros((EXTRA - 3, 384), F32)], 0
    ).astype(BF16)
    row = jnp.concatenate([row, jnp.zeros((EXTRA, 640), BF16)], 1)
    for pair in range(8):
        both = jnp.concatenate(
            [in_ref[2 * pair, pl.ds(0, 64), :], in_ref[2 * pair + 1, pl.ds(0, 64), :]], 0
        ).T
        for y in range(4):
            for x in range(4):
                out_ref[y * 4 + x, pl.ds(0, 32), pl.ds(pair * 128, 128)] = both[
                    y * 32 : y * 32 + 32
                ]
    for block in range(16):
        out_ref[block, pl.ds(32, EXTRA), :] = row


def normalise(place_ref, alive_total_ref, in_ref, all_ref, enc_ref, dec_ref, loss_ref):
    x_own = place_ref[4]
    riders = jnp.zeros((EXTRA, 384), F32)
    for y in range(4):
        riders = riders + in_ref[y * 4 + x_own, pl.ds(32, EXTRA), pl.ds(0, 384)].astype(F32)
    riders = riders[0:1] + riders[1:2] + riders[2:3]
    loss_ref[...] = riders[:, :256] * (1.0 / 4096.0)
    mean_norm = riders[:, 256:257] / alive_total_ref[0]
    gain = ENC_GAIN * mean_norm
    slot = lax.broadcasted_iota(jnp.int32, (32, 1), 0)
    for x in range(4):
        squares = jnp.zeros((32, 1), F32)
        for y in range(4):
            rows = in_ref[y * 4 + x, pl.ds(0, 32), :].astype(F32)
            squares = squares + jnp.sum(rows * rows, axis=1, keepdims=True)
        valid = jnp.where(slot < place_ref[x], 1.0, 0.0)
        scale = lax.rsqrt(squares + EPSILON) * valid
        for y in range(4):
            cols = pl.ds(y * 1024, 1024)
            unit = in_ref[y * 4 + x, pl.ds(0, 32), :].astype(F32) * scale
            row = (gain * unit).astype(BF16)
            all_ref[pl.ds(x * 32, 32), cols] = row

            @pl.when(x == x_own)
            def _(unit=unit, row=row, cols=cols):
                enc_ref[:, cols] = row
                dec_ref[:, cols] = unit.astype(BF16)


def reencode(place_ref, mine_ref, other_ref, tokens_ref, out_ref, rows_ref):
    core = place_ref[5]
    for x in range(4):
        part = pl.ds(x * 32, 32)
        rows_ref[pl.ds(pl.multiple_of(x * 64 + core * 32, 32), 32), :] = mine_ref[part, :]
        rows_ref[pl.ds(pl.multiple_of(x * 64 + 32 - core * 32, 32), 32), :] = other_ref[part, :]
    product = lax.dot_general(
        tokens_ref[...],
        rows_ref[...],
        (((1,), (1,)), ((), ())),
        preferred_element_type=F32,
    )
    out_ref[...] = jnp.maximum(product, 0.0).astype(BF16)


def exchange(value, axes):
    return lax.all_to_all(value, axes, 0, 0, tiled=True)


def on_device(acts, dec_bias, enc_weight, enc_bias, dec_weight, dead_ids, tile_count, sample_rows):
    z_index = lax.axis_index("z")
    y_index = lax.axis_index("y")
    x_index = lax.axis_index("x")
    core_index = lax.axis_index("core")
    feat_index = z_index * 4 + y_index
    width, latents = enc_weight.shape
    tokens = acts.shape[1]
    tile = sample_rows.shape[2]
    slots = dead_ids.shape[1]
    depth = acts.shape[0]

    centered = (acts.astype(F32) - dec_bias[:, None]).astype(BF16)
    by_z = exchange(jnp.broadcast_to(centered[None], (16, depth, tokens)), "z")
    by_z = by_z.reshape(1, 16 * depth, tokens)
    gathered = exchange(jnp.broadcast_to(by_z, (4, 16 * depth, tokens)), "y")
    gathered = gathered.reshape(width, tokens)

    counts = lax.dynamic_index_in_dim(tile_count, feat_index, 0, keepdims=False)
    slot = jnp.arange(slots, dtype=jnp.int32)
    valid = (slot % tile) < jnp.repeat(counts, tile)
    hits = (dead_ids[0][:, None] == jnp.arange(latents, dtype=jnp.int32)[None, :]) & valid[:, None]
    alive = 1.0 - jnp.any(hits, axis=0).astype(F32)
    alive_total = (64 * latents - jnp.sum(tile_count)).astype(F32).reshape(1)

    enc_t, dec_t, onehot, stat = kernel_call(
        prepare,
        (
            jax.ShapeDtypeStruct((latents, width), BF16),
            jax.ShapeDtypeStruct((width, latents), BF16),
            jax.ShapeDtypeStruct((tokens, 64 * tile), BF16),
            jax.ShapeDtypeStruct((1, 1), F32),
        ),
        [VM] * 4,
        1 << 24,
        9 << 20,
    )(enc_weight, dec_weight, alive[None, :], sample_rows.reshape(1, 64 * tile))

    recon = kernel_call(
        forward,
        jax.ShapeDtypeStruct((width, tokens), BF16),
        [VM] * 5,
        4 * width * latents * tokens,
        8 << 20,
    )(enc_t, gathered, enc_bias[:, None], alive[:, None], dec_t)
    by_token = kernel_call(
        turn, jax.ShapeDtypeStruct((tokens, width), BF16), [VM], 1 << 22, 4 << 20
    )(gathered)

    part = exchange(recon.reshape(4, width // 4, tokens), "y")
    part = jnp.sum(part.astype(F32), axis=0).astype(BF16)
    part = exchange(part.reshape(16, depth, tokens), "z")

    source = y_index * 16 + z_index
    own = lax.dynamic_index_in_dim(
        gathered.reshape(64, depth, tokens),
        (source % 4) * 16 + source // 4,
        0,
        keepdims=False,
    )
    picks = kernel_call(
        residual,
        jax.ShapeDtypeStruct((16, depth + EXTRA, 4 * tile), BF16),
        [VM] * 4,
        2 * depth * tokens * 64 * tile,
        2 << 20,
    )(part, own, onehot, stat)
    picks = exchange(picks, "z")
    picks = kernel_call(
        relay,
        jax.ShapeDtypeStruct((16, tile + EXTRA, width // 4), BF16),
        [VM],
        1 << 20,
        2 << 20,
    )(picks)
    picks = exchange(picks, ("y", "x"))

    places = jnp.concatenate(
        [
            lax.dynamic_index_in_dim(counts.reshape(4, 2), core_index, 1, keepdims=False),
            x_index[None],
            core_index[None],
        ]
    ).astype(jnp.int32)
    mine, new_enc, new_dec, token_loss = kernel_call(
        normalise,
        (
            jax.ShapeDtypeStruct((4 * tile, width), BF16),
            jax.ShapeDtypeStruct((tile, width), BF16),
            jax.ShapeDtypeStruct((tile, width), BF16),
            jax.ShapeDtypeStruct((1, tokens), F32),
        ),
        [SM, SM, VM],
        1 << 22,
        3 << 20,
    )(places, alive_total, picks)
    other = lax.ppermute(mine, "core", [(0, 1), (1, 0)])
    reencoded = kernel_call(
        reencode,
        jax.ShapeDtypeStruct((tokens, slots), BF16),
        [SM, VM, VM, VM],
        2 * tokens * slots * width,
        5 << 20,
        [pltpu.VMEM((slots, width), BF16)],
    )(places, mine, other, by_token)
    return (new_enc, new_dec, reencoded, token_loss.reshape(tokens))


def solution(mesh):
    fine = Mesh(mesh.devices.reshape(16, 4, 4, 2), ("z", "y", "x", "core"))
    feat, tok = ("z", "y"), ("x", "core")
    in_specs = (
        P(feat, tok),
        P(feat),
        P(None, feat),
        P(feat),
        P(feat, None),
        P(feat, None),
        P(),
        P(None, tok, None),
    )
    out_specs = (P(feat + tok, None), P(feat + tok, None), P(tok, feat), P(tok))
    return jax.shard_map(
        on_device, mesh=fine, in_specs=in_specs, out_specs=out_specs, check_vma=False
    )
```

time: 648 us -> 215 us (0.33)
  waiting for transfers between devices: 482 us -> 47.6 us
  starting transfers between devices: 0.16 us -> 46.3 us
  blocking collectives: 115 us -> 85.5 us
  between operations: 15.8 us -> 1.49 us
  Pallas kernels: 0 us -> 11.3 us
  matrix products: 10.2 us -> 0 us
    unnamed x5 -> x0, waiting for transfers between devices: 284 us -> none
    all_gather x3 -> x0, waiting for transfers between devices: 198 us -> none  [the longest x1 136 us: on_device(): piece = lax.all_gather(centered_local, 'feat', axis=0, tiled=True)]
    psum x1 -> x0, blocking collectives: 115 us -> none  [on_device(): stat_sum = lax.psum(stat_local, 'feat')]
    all_to_all x0 -> x3, blocking collectives: none -> 85.5 us  [exchange(): return lax.all_to_all(value, axes, 0, 0, tiled=True)]
    all_to_all x0 -> x3, waiting for transfers between devices: none -> 46 us  [exchange(): return lax.all_to_all(value, axes, 0, 0, tiled=True)]
    all_to_all x0 -> x3, starting transfers between devices: none -> 35.4 us  [exchange(): return lax.all_to_all(value, axes, 0, 0, tiled=True)]
    pallas_call x0 -> x7, Pallas kernels: none -> 11.3 us  [the longest x1 3.02 us: on_device(): kernel_call(normalise, (jax.ShapeDtypeStruct((4 * tile, width), BF16), ja...]
    ppermute x0 -> x1, starting transfers between devices: none -> 10.9 us  [on_device(): other = lax.ppermute(mine, 'core', [(0, 1), (1, 0)])]
  transfers between devices with their start and end apart: 4 -> 4, of which waited for: 4 -> 4; matrix products, arithmetic and copies ran while one was open for 1% -> 1% of each run, Pallas kernels for 0% -> 1%
where the time goes in v1:
time: 215 us; the launch traced here: 212 us
  blocking collectives  85.5 us (40%)
  waiting for transfers between devices  47.6 us (22%)
  starting transfers between devices  46.3 us (22%)
  local copies, waits for them, and re-layouts  15 us (7%)
  Pallas kernels  11.3 us (5%)
  other arithmetic  4.55 us (2%)
    all_to_all x3, blocking collectives, exchange(): return lax.all_to_all(value, axes, 0, 0, tiled=True)  85.5 us
    all_to_all x3, waiting for transfers between devices, exchange(): return lax.all_to_all(value, axes, 0, 0, tiled=True)  46 us
    all_to_all x3, starting transfers between devices, exchange(): return lax.all_to_all(value, axes, 0, 0, tiled=True)  35.4 us
    unnamed x27, local copies, waits for them, and re-layouts  12.5 us
    ppermute x1, starting transfers between devices, on_device(): other = lax.ppermute(mine, 'core', [(0, 1), (1, 0)])  10.9 us
  transfers between devices with their start and end apart: 4, of which 4 were waited for; matrix products, arithmetic and copies ran while one was open for 1% of the time, Pallas kernels for 1%

profile of v1, /device:TPU:1, one launch (start us, length us, event | category | flops | bytes accessed | tf_op | source)
XLA Modules:
  0.0 211.7 jit_solution(2333269071593867501)
XLA Ops:
  0.6 0.8 subtract_convert_fusion
  1.5 38.4 %all_to_all.30 = bf16[16,64,256]{2,1,0:T(8,128)(2,1)S(1)} all-to-all(bf16[16,64,256]{2,1,0:T(8,128)(2,1)S(1)} %broadcast_in_dim.33), channel_id=1, replica_groups=mesh['z'=16,'y'=4,'x'=4,'core'=2] {'z'}, dimensions={0} | all-to-all | bytes 1048576 | tf_op jit(solution)/shard_map/all_to_all | solution.py:177
  39.9 1.4 broadcast_in_dim.35
  41.4 4.3 %all-to-all-start.1 = ((bf16[4,1024,256]{2,1,0:T(8,128)(2,1)}), bf16[4,1024,256]{2,1,0:T(8,128)(2,1)S(1)}, u32[]{:S(2)}, u32[]{:S(2)}) async-start(bf16[4,1024,256]{2,1,0:T(8,128)(2,1)} %broadcast_in_dim.35), calls=%async_computation.1 | async-start | bytes 4194304 | tf_op jit(solution)/shard_map/all_to_all | solution.py:177
  45.7 0.0 copy-done.10
  45.7 0.2 dynamic-slice_reduce_fusion
  45.9 0.1 broadcast_in_dim.32
  45.9 0.1 reshape.80
  46.0 0.0 copy-done.9
  46.0 0.1 copy.16
  46.1 0.1 reshape.81.rows_ref
  46.2 0.0 copy-done.11
  46.2 0.1 copy.17.bias_ref
  46.4 0.0 copy-done.12
  46.4 0.2 fusion.1
  46.5 0.1 copy.18.alive_ref
  46.7 0.0 copy-start.1
  46.7 1.6 copy-done.1
  48.3 1.6 copy-done.2
  49.9 1.8 shard_map.111
  51.7 1.3 copy-done.3
  53.0 1.3 copy-done.5
  54.4 1.0 copy-done.7
  55.4 8.9 %all-to-all-done.1 = bf16[4,1024,256]{2,1,0:T(8,128)(2,1)S(1)} async-done(((bf16[4,1024,256]{2,1,0:T(8,128)(2,1)}), bf16[4,1024,256]{2,1,0:T(8,128)(2,1)S(1)}, u32[]{:S(2)}, u32[]{:S(2)}) %all-to-all-start.1) | async-done | bytes 2097184 | tf_op jit(solution)/shard_map/all_to_all | solution.py:177
  64.2 1.6 copy-done.4
  65.8 1.6 copy-done.6
  67.4 2.4 %shard_map.112 = bf16[4096,256]{1,0:T(8,128)(2,1)S(1)} custom-call(bf16[256,4096]{1,0:T(8,128)(2,1)S(1)} %copy-done.4, bf16[4096,256]{1,0:T(8,128)(2,1)S(1)} %bitcast.17, f32[256,1]{1,0:T(8,128)S(1)} %copy.17.bias_ref, f32[256,1]{1,0:T(8,128)S(1)} %copy.18.alive_ref, bf16[4096,256]{1,0:T(8,128)(2,1)S(1)} %copy-done.6), custom_call_target="tpu_custom_call" | custom-call | flops 1073741824 | bytes 8388608 | tf_op jit(solution)/shard_map/pallas_call | solution.py:218
  69.9 20.9 %all_to_all.31 = bf16[4,1024,256]{2,1,0:T(8,128)(2,1)} all-to-all(bf16[4,1024,256]{2,1,0:T(8,128)(2,1)S(1)} %bitcast.20), channel_id=1, replica_groups=mesh['z'=16,'y'=4,'x'=4,'core'=2] {'y'}, dimensions={0} | all-to-all | bytes 4194304 | tf_op jit(solution)/shard_map/all_to_all | solution.py:177
  90.7 2.8 %reduce_sum.22 = bf16[1024,256]{1,0:T(8,128)(2,1)} reduce(bf16[4,1024,256]{2,1,0:T(8,128)(2,1)} %all_to_all.31, bf16[]{:T(256)} %constant.78.clone.1), dimensions={0}, to_apply=%region_2.3 | reduce | flops 786432 | bytes 2621442 | tf_op jit(solution)/shard_map/reduce_sum | solution.py:230
  93.6 26.3 %all-to-all-start.3 = ((bf16[16,64,256]{2,1,0:T(8,128)(2,1)}), bf16[16,64,256]{2,1,0:T(8,128)(2,1)S(1)}, u32[]{:S(2)}, u32[]{:S(2)}) async-start(bf16[16,64,256]{2,1,0:T(8,128)(2,1)} %bitcast.10), calls=%async_computation.3 | async-start | bytes 1048576 | tf_op jit(solution)/shard_map/all_to_all | solution.py:177
  120.0 21.3 %all-to-all-done.3.part_ref = bf16[16,64,256]{2,1,0:T(8,128)(2,1)S(1)} async-done(((bf16[16,64,256]{2,1,0:T(8,128)(2,1)}), bf16[16,64,256]{2,1,0:T(8,128)(2,1)S(1)}, u32[]{:S(2)}, u32[]{:S(2)}) %all-to-all-start.3) | async-done | bytes 524320 | tf_op jit(solution)/shard_map/all_to_all | solution.py:177
  141.3 1.2 copy-done.8
  142.5 1.0 shard_map.113
  143.5 26.3 %all_to_all.32.in_ref = bf16[16,80,128]{2,1,0:T(8,128)(2,1)S(1)} all-to-all(bf16[16,80,128]{2,1,0:T(8,128)(2,1)S(1)} %shard_map.113), channel_id=1, replica_groups=mesh['z'=16,'y'=4,'x'=4,'core'=2] {'z'}, dimensions={0} | all-to-all | bytes 655360 | tf_op jit(solution)/shard_map/all_to_all | solution.py:177
  169.8 0.3 shard_map.114
  170.0 0.0 copy-start
  170.1 1.1 copy-done
  171.2 4.8 %all-to-all-start.5 = ((bf16[16,48,1024]{2,1,0:T(8,128)(2,1)}), bf16[16,48,1024]{2,1,0:T(8,128)(2,1)}, u32[]{:S(2)}, u32[]{:S(2)}) async-start(bf16[16,48,1024]{2,1,0:T(8,128)(2,1)} %copy-done), calls=%async_computation.5 | async-start | bytes 3145728 | tf_op jit(solution)/shard_map/all_to_all | solution.py:177
  176.0 0.1 reshape.78
  176.1 0.6 reduce_sum.21
  177.3 0.2 dynamic-slice_reduce_fusion.1
  177.5 0.1 pad_add_fusion.place_ref
  177.6 15.8 %all-to-all-done.5.in_ref = bf16[16,48,1024]{2,1,0:T(8,128)(2,1)} async-done(((bf16[16,48,1024]{2,1,0:T(8,128)(2,1)}), bf16[16,48,1024]{2,1,0:T(8,128)(2,1)}, u32[]{:S(2)}, u32[]{:S(2)}) %all-to-all-start.5) | async-done | bytes 1572896 | tf_op jit(solution)/shard_map/all_to_all | solution.py:177
  193.4 3.0 %shard_map.115 = (bf16[128,4096]{1,0:T(8,128)(2,1)S(1)}, bf16[32,4096]{1,0:T(8,128)(2,1)}, bf16[32,4096]{1,0:T(8,128)(2,1)}, f32[1,256]{1,0:T(1,128)}) custom-call(s32[6]{0:T(128)S(1)} %pad_add_fusion.place_ref, f32[1]{0:T(128)} %bitcast.2.alive_total_ref, bf16[16,48,1024]{2,1,0:T(8,128)(2,1)} %all-to-all-done.5.in_ref), custom_call_target="tpu_custom_call" | custom-call | flops 4194304 | bytes 3145728 | tf_op jit(solution)/shard_map/pallas_call | solution.py:264
  196.5 10.9 %collective-permute-start = (bf16[128,4096]{1,0:T(8,128)(2,1)S(1)}, bf16[128,4096]{1,0:T(8,128)(2,1)S(1)}, u32[]{:S(2)}, u32[]{:S(2)}) collective-permute-start(bf16[128,4096]{1,0:T(8,128)(2,1)S(1)} %get-tuple-element.18.mine_ref), channel_id=1, source_target_pairs={{0,1},{1,0},{2,3},{3,2},{4,5},{5,4},{6,7},{7,6},{8,9},{9,8},{10,11... | collective-permute-start | bytes 3145736 | tf_op jit(solution)/shard_map/ppermute | solution.py:276
  207.3 0.7 shard_map.116.tokens_ref
  208.0 1.6 collective-permute-done.other_ref
  209.6 2.1 shard_map.117
  (15 shorter events, 0.1 us)
Async XLA Ops:
  41.3 4.3 %copy-start.10 = (s32[64,8]{0,1:T(8,128)S(1)}, s32[64,8]{0,1:T(8,128)}, u32[]{:S(2)}) copy-start(s32[64,8]{0,1:T(8,128)} %param.14) | copy-start | bytes 6148
  41.3 4.7 %copy-start.9 = (s32[64,1,32]{0,2,1:T(8,128)S(1)}, s32[64,1,32]{0,2,1:T(8,128)}, u32[]{:S(2)}) copy-start(s32[64,1,32]{0,2,1:T(8,128)} %param.15) | copy-start | bytes 24580
  41.3 4.9 %copy-start.11 = (f32[256]{0:T(256)S(1)}, f32[256]{0:T(256)}, u32[]{:S(2)}) copy-start(f32[256]{0:T(256)} %param.11) | copy-start | bytes 3076
  41.3 5.0 %copy-start.12 = (s32[1,256]{1,0:T(1,128)S(1)}, s32[1,256]{1,0:T(1,128)}, u32[]{:S(2)}) copy-start(s32[1,256]{1,0:T(1,128)} %param.13) | copy-start | bytes 3076
  41.4 22.9 %all-to-all-start.1 = ((bf16[4,1024,256]{2,1,0:T(8,128)(2,1)}), bf16[4,1024,256]{2,1,0:T(8,128)(2,1)S(1)}, u32[]{:S(2)}, u32[]{:S(2)}) async-start(bf16[4,1024,256]{2,1,0:T(8,128)(2,1)} %broadcast_in_dim.35), calls=%async_computation.1 | async-start | bytes 4194304 | tf_op jit(solution)/shard_map/all_to_all | solution.py:177
  46.7 1.6 copy-start.1
  48.3 1.6 copy-start.2
  51.7 1.3 copy-start.3
  53.0 1.3 copy-start.5
  54.4 1.0 copy-start.7
  64.2 1.6 copy-start.4
  65.8 1.6 copy-start.6
  93.6 47.7 %all-to-all-start.3 = ((bf16[16,64,256]{2,1,0:T(8,128)(2,1)}), bf16[16,64,256]{2,1,0:T(8,128)(2,1)S(1)}, u32[]{:S(2)}, u32[]{:S(2)}) async-start(bf16[16,64,256]{2,1,0:T(8,128)(2,1)} %bitcast.10), calls=%async_computation.3 | async-start | bytes 1048576 | tf_op jit(solution)/shard_map/all_to_all | solution.py:177
  141.3 1.2 copy-start.8
  170.0 1.2 copy-start
  171.2 22.2 %all-to-all-start.5 = ((bf16[16,48,1024]{2,1,0:T(8,128)(2,1)}), bf16[16,48,1024]{2,1,0:T(8,128)(2,1)}, u32[]{:S(2)}, u32[]{:S(2)}) async-start(bf16[16,48,1024]{2,1,0:T(8,128)(2,1)} %copy-done), calls=%async_computation.5 | async-start | bytes 3145728 | tf_op jit(solution)/shard_map/all_to_all | solution.py:177
  196.5 13.2 %collective-permute-start = (bf16[128,4096]{1,0:T(8,128)(2,1)S(1)}, bf16[128,4096]{1,0:T(8,128)(2,1)S(1)}, u32[]{:S(2)}, u32[]{:S(2)}) collective-permute-start(bf16[128,4096]{1,0:T(8,128)(2,1)S(1)} %get-tuple-element.18.mine_ref), channel_id=1, source_target_pairs={{0,1},{1,0},{2,3},{3,2},{4,5},{5,4},{6,7},{7,6},{8,9},{9,8},{10,11... | collective-permute-start | bytes 3145736 | tf_op jit(solution)/shard_map/ppermute | solution.py:276

commit v2 on v1

v2 whole, which is shorter than its diff:
```python
import jax
import jax.numpy as jnp
from jax import lax
from jax.experimental import pallas as pl
from jax.experimental.pallas import tpu as pltpu
from jax.sharding import Mesh, PartitionSpec as P

ENC_GAIN = 0.2
EPSILON = 1e-06
F32 = jnp.float32
BF16 = jnp.bfloat16
VM = pl.BlockSpec(memory_space=pltpu.VMEM)
SM = pl.BlockSpec(memory_space=pltpu.SMEM)
EXTRA = 16


def kernel_call(body, out_shape, in_specs, flops, mib, scratch=()):
    multi = isinstance(out_shape, (tuple, list))
    return pl.pallas_call(
        body,
        out_shape=out_shape,
        in_specs=in_specs,
        out_specs=[VM] * len(out_shape) if multi else VM,
        scratch_shapes=list(scratch),
        compiler_params=pltpu.CompilerParams(vmem_limit_bytes=(mib + 4) << 20),
        cost_estimate=pl.CostEstimate(
            flops=flops, bytes_accessed=mib << 20, transcendentals=0
        ),
    )


def split3(v):
    hi = v.astype(BF16)
    rest = v - hi.astype(F32)
    mid = rest.astype(BF16)
    lo = (rest - mid.astype(F32)).astype(BF16)
    return hi, mid, lo


def spread(in_ref, out_ref):
    for y in range(4):
        out_ref[y] = in_ref[...]


def prepare(
    count_ref,
    enc_ref,
    dec_ref,
    bias_ref,
    dead_ref,
    sample_ref,
    enc_t_ref,
    dec_t_ref,
    onehot_ref,
    bias_t_ref,
    alive_ref,
    stat_ref,
):
    latents = enc_ref.shape[1]
    feat = lax.axis_index("z") * 4 + lax.axis_index("y")
    total = jnp.zeros((1, latents), F32)
    for y in range(4):
        for pair in range(8):
            parts = []
            for z in (2 * pair, 2 * pair + 1):
                block = enc_ref[pl.ds((z * 4 + y) * 64, 64), :]
                wide = block.astype(F32)
                total = total + jnp.sum(wide * wide, axis=0, keepdims=True)
                parts.append(block)
            enc_t_ref[:, pl.ds(y * 1024 + pair * 128, 128)] = jnp.concatenate(parts, 0).T
    for block in range(16):
        dec_t_ref[pl.ds(block * 256, 256), :] = dec_ref[:, pl.ds(block * 256, 256)].T

    row = lax.broadcasted_iota(jnp.int32, (latents, latents), 0)
    col = lax.broadcasted_iota(jnp.int32, (latents, latents), 1)
    slot = lax.broadcasted_iota(jnp.int32, (1, latents), 1)
    limit = jnp.zeros((1, latents), jnp.int32)
    for t in range(8):
        limit = jnp.where(slot // 32 == t, count_ref[feat, t], limit)
    dead = jnp.where(slot % 32 < limit, dead_ref[...], -1)
    hit = jnp.where(dead == row, 1.0, 0.0)
    alive = 1.0 - jnp.max(hit, axis=1, keepdims=True)
    alive_ref[...] = alive
    bias_t_ref[...] = jnp.sum(jnp.where(row == col, bias_ref[...], 0.0), axis=1, keepdims=True)
    norms = jnp.sum(jnp.where(row == col, jnp.sqrt(total), 0.0), axis=1, keepdims=True)
    stat_ref[...] = jnp.sum(norms * alive, axis=0, keepdims=True)

    tokens = onehot_ref.shape[0]
    sample = sample_ref[...]
    shard = lax.broadcasted_iota(jnp.int32, sample.shape, 1)
    wide = jnp.concatenate([jnp.where(shard % 4 == y, sample, 0) for y in range(4)], 0)
    wide = jnp.concatenate([wide, jnp.zeros_like(wide)], 1).T
    token = lax.broadcasted_iota(jnp.int32, (tokens, 128), 0)
    for z in range(16):
        wanted = jnp.sum(wide[z * 4 : z * 4 + 4], axis=0, keepdims=True)
        onehot_ref[:, pl.ds(z * 128, 128)] = jnp.where(token == wanted, 1.0, 0.0).astype(BF16)


def fold(in_ref, out_ref):
    for block in range(8):
        rows = pl.ds(block * 128, 128)
        total = in_ref[0, rows, :].astype(F32)
        for y in range(1, 4):
            total = total + in_ref[y, rows, :].astype(F32)
        out_ref[rows, :] = total.astype(BF16)


def turn(g_ref, after_ref, out_ref):
    for z in range(16):
        for pair in range(2):
            y = 2 * pair
            both = jnp.concatenate(
                [
                    g_ref[pl.ds((y * 16 + z) * 64, 64), :],
                    g_ref[pl.ds(((y + 1) * 16 + z) * 64, 64), :],
                ],
                0,
            )
            out_ref[:, pl.ds(z * 256 + pair * 128, 128)] = both.T


def forward(enc_t_ref, g_ref, bias_ref, alive_ref, dec_t_ref, out_ref):
    pre = jnp.dot(enc_t_ref[...], g_ref[...], preferred_element_type=F32)
    feat = (jnp.maximum(pre + bias_ref[...], 0.0) * alive_ref[...]).astype(BF16)
    for block in range(16):
        rows = pl.ds(block * 256, 256)
        out_ref[rows, :] = jnp.dot(
            dec_t_ref[rows, :], feat, preferred_element_type=F32
        ).astype(BF16)


def residual(part_ref, g_ref, onehot_ref, stat_ref, out_ref):
    source = lax.axis_index("y") * 16 + lax.axis_index("z")
    own = g_ref[(source % 4) * 16 + source // 4]
    recon = part_ref[0].astype(F32)
    for z in range(1, 16):
        recon = recon + part_ref[z].astype(F32)
    error = own.astype(F32) - recon
    loss = jnp.sum(error * error, axis=0, keepdims=True)
    loss = jnp.concatenate([loss[:, :128], loss[:, 128:]], 0)
    stat = jnp.broadcast_to(stat_ref[...], (2, 128))
    pad = jnp.zeros((4, 128), F32)
    pieces = [split3(v) for v in (loss, stat)]
    extra = jnp.concatenate([p.astype(F32) for s in pieces for p in s] + [pad], 0).astype(BF16)
    error_b = error.astype(BF16)
    for z in range(16):
        picked = jnp.dot(
            error_b, onehot_ref[:, pl.ds(z * 128, 128)], preferred_element_type=F32
        )
        out_ref[z, pl.ds(0, 64), :] = picked.astype(BF16)
        out_ref[z, pl.ds(64, EXTRA), :] = extra


def relay(in_ref, out_ref):
    riders = in_ref[0, pl.ds(64, EXTRA), :].astype(F32)
    hi, mid, lo = riders[0:2], riders[2:4], riders[4:6]
    shi, smid, slo = riders[6:8], riders[8:10], riders[10:12]
    loss = hi + mid + lo
    stat = shi + smid + slo
    for z in range(1, 16):
        riders = in_ref[z, pl.ds(64, EXTRA), :].astype(F32)
        loss = loss + (riders[0:2] + riders[2:4] + riders[4:6])
        stat = stat + (riders[6:8] + riders[8:10] + riders[10:12])
    row = jnp.concatenate([loss[0:1], loss[1:2], stat[0:1]], 1)
    row = jnp.concatenate(
        [p.astype(F32) for p in split3(row)] + [jnp.zeros((EXTRA - 3, 384), F32)], 0
    ).astype(BF16)
    row = jnp.concatenate([row, jnp.zeros((EXTRA, 640), BF16)], 1)
    for pair in range(8):
        both = jnp.concatenate(
            [in_ref[2 * pair, pl.ds(0, 64), :], in_ref[2 * pair + 1, pl.ds(0, 64), :]], 0
        ).T
        for y in range(4):
            for x in range(4):
                out_ref[y * 4 + x, pl.ds(0, 32), pl.ds(pair * 128, 128)] = both[
                    y * 32 : y * 32 + 32
                ]
    for block in range(16):
        out_ref[block, pl.ds(32, EXTRA), :] = row


def normalise(count_ref, counts_ref, in_ref, all_ref, enc_ref, dec_ref, loss_ref):
    feat = lax.axis_index("z") * 4 + lax.axis_index("y")
    x_own = lax.axis_index("x")
    core = lax.axis_index("core")
    riders = jnp.zeros((EXTRA, 384), F32)
    for y in range(4):
        riders = riders + in_ref[y * 4 + x_own, pl.ds(32, EXTRA), pl.ds(0, 384)].astype(F32)
    riders = riders[0:1] + riders[1:2] + riders[2:3]
    loss_ref[...] = riders[:, :256] * (1.0 / 4096.0)
    dead = jnp.sum(counts_ref[...].astype(F32), axis=0, keepdims=True)
    dead = jnp.sum(dead, axis=1, keepdims=True)
    gain = ENC_GAIN * (riders[:, 256:257] / (16384.0 - dead))
    slot = lax.broadcasted_iota(jnp.int32, (32, 1), 0)
    for x in range(4):
        squares = jnp.zeros((32, 1024), F32)
        for y in range(4):
            rows = in_ref[y * 4 + x, pl.ds(0, 32), :].astype(F32)
            squares = squares + rows * rows
        squares = jnp.sum(squares, axis=1, keepdims=True)
        valid = jnp.where(slot < count_ref[feat, x * 2 + core], 1.0, 0.0)
        scale = lax.rsqrt(squares + EPSILON) * valid
        for y in range(4):
            unit = in_ref[y * 4 + x, pl.ds(0, 32), :].astype(F32) * scale
            all_ref[pl.ds(x * 32, 32), pl.ds(y * 1024, 1024)] = (gain * unit).astype(BF16)

        @pl.when(x == x_own)
        def _(scale=scale, x=x):
            for y in range(4):
                cols = pl.ds(y * 1024, 1024)
                unit = in_ref[y * 4 + x, pl.ds(0, 32), :].astype(F32) * scale
                enc_ref[:, cols] = (gain * unit).astype(BF16)
                dec_ref[:, cols] = unit.astype(BF16)


def reencode(mine_ref, other_ref, tokens_ref, out_ref, rows_ref):
    core = lax.axis_index("core")
    for x in range(4):
        part = pl.ds(x * 32, 32)
        rows_ref[pl.ds(pl.multiple_of(x * 64 + core * 32, 32), 32), :] = mine_ref[part, :]
        rows_ref[pl.ds(pl.multiple_of(x * 64 + 32 - core * 32, 32), 32), :] = other_ref[part, :]
    product = lax.dot_general(
        tokens_ref[...],
        rows_ref[...],
        (((1,), (1,)), ((), ())),
        preferred_element_type=F32,
    )
    out_ref[...] = jnp.maximum(product, 0.0).astype(BF16)


def exchange(value, axes):
    return lax.all_to_all(value, axes, 0, 0, tiled=True)


def shape(*dims, dtype=BF16):
    return jax.ShapeDtypeStruct(dims, dtype)


def on_device(acts, dec_bias, enc_weight, enc_bias, dec_weight, dead_ids, tile_count, sample_rows):
    width, latents = enc_weight.shape
    depth, tokens = acts.shape
    tile = sample_rows.shape[2]
    slots = dead_ids.shape[1]

    centered = (acts.astype(F32) - dec_bias[:, None]).astype(BF16)
    by_z = exchange(jnp.broadcast_to(centered[None], (16, depth, tokens)), "z")
    by_z = by_z.reshape(16 * depth, tokens)
    by_z = kernel_call(spread, shape(4, 16 * depth, tokens), [VM], 1 << 20, 3)(by_z)
    gathered = exchange(by_z, "y").reshape(width, tokens)

    enc_t, dec_t, onehot, bias_t, alive, stat = kernel_call(
        prepare,
        (
            shape(latents, width),
            shape(width, latents),
            shape(tokens, 64 * tile),
            shape(latents, 1, dtype=F32),
            shape(latents, 1, dtype=F32),
            shape(1, 1, dtype=F32),
        ),
        [SM] + [VM] * 5,
        1 << 24,
        9,
    )(
        tile_count,
        enc_weight,
        dec_weight,
        enc_bias.reshape(1, latents),
        dead_ids,
        sample_rows.transpose(1, 2, 0).reshape(tile, 64),
    )

    recon = kernel_call(
        forward, shape(width, tokens), [VM] * 5, 4 * width * latents * tokens, 8
    )(enc_t, gathered, bias_t, alive, dec_t)

    part = exchange(recon.reshape(4, width // 4, tokens), "y")
    part = kernel_call(fold, shape(width // 4, tokens), [VM], 1 << 20, 3)(part)
    part = exchange(part.reshape(16, depth, tokens), "z")

    picks = kernel_call(
        residual,
        shape(16, depth + EXTRA, 4 * tile),
        [VM] * 4,
        2 * depth * tokens * 64 * tile,
        4,
    )(part, gathered.reshape(64, depth, tokens), onehot, stat)
    picks = exchange(picks, "z")
    picks = kernel_call(relay, shape(16, tile + EXTRA, width // 4), [VM], 1 << 20, 2)(picks)
    picks = exchange(picks, ("y", "x"))
    mine, new_enc, new_dec, token_loss = kernel_call(
        normalise,
        (
            shape(4 * tile, width),
            shape(tile, width),
            shape(tile, width),
            shape(1, tokens, dtype=F32),
        ),
        [SM, VM, VM],
        1 << 22,
        4,
    )(tile_count, tile_count, picks)
    by_token = kernel_call(turn, shape(tokens, width), [VM, VM], 1 << 22, 4)(gathered, token_loss)
    other = lax.ppermute(mine, "core", [(0, 1), (1, 0)])
    reencoded = kernel_call(
        reencode,
        shape(tokens, slots),
        [VM, VM, VM],
        2 * tokens * slots * width,
        7,
        [pltpu.VMEM((slots, width), BF16)],
    )(mine, other, by_token)
    return (new_enc, new_dec, reencoded, token_loss.reshape(tokens))


def solution(mesh):
    fine = Mesh(mesh.devices.reshape(16, 4, 4, 2), ("z", "y", "x", "core"))
    feat, tok = ("z", "y"), ("x", "core")
    in_specs = (
        P(feat, tok),
        P(feat),
        P(None, feat),
        P(feat),
        P(feat, None),
        P(feat, None),
        P(),
        P(None, tok, None),
    )
    out_specs = (P(feat + tok, None), P(feat + tok, None), P(tok, feat), P(tok))
    return jax.shard_map(
        on_device, mesh=fine, in_specs=in_specs, out_specs=out_specs, check_vma=False
    )
```

time: 215 us -> 206 us (0.958)
  blocking collectives: 85.5 us -> 152 us
  waiting for transfers between devices: 47.6 us -> 10.2 us
  starting transfers between devices: 46.3 us -> 15.8 us
  local copies, waits for them, and re-layouts: 15 us -> 11.2 us
  other arithmetic: 4.55 us -> 0.84 us
    all_to_all x3 -> x5, blocking collectives: 85.5 us -> 152 us  [exchange(): return lax.all_to_all(value, axes, 0, 0, tiled=True)]
    all_to_all x3 -> x1, waiting for transfers between devices: 46 us -> 9.31 us  [exchange(): return lax.all_to_all(value, axes, 0, 0, tiled=True)]
    all_to_all x3 -> x1, starting transfers between devices: 35.4 us -> 4.33 us  [exchange(): return lax.all_to_all(value, axes, 0, 0, tiled=True)]
    reduce_sum x2 -> x0, other arithmetic: 3.47 us -> none  [the longest x1 2.84 us: on_device(): part = jnp.sum(part.astype(F32), axis=0).astype(BF16)]
    unnamed x27 -> x25, local copies, waits for them, and re-layouts: 12.5 us -> 11.1 us
    pallas_call x7 -> x9, Pallas kernels: 11.3 us -> 12.4 us  [the longest x1 3.28 us: on_device(): kernel_call(prepare, (shape(latents, width), shape(width, latents), shape...]
  transfers between devices with their start and end apart: 4 -> 2, of which waited for: 4 -> 2; matrix products, arithmetic and copies ran while one was open for 1% -> 0% of each run, Pallas kernels for 1% -> 2%
where the time goes in v2:
time: 206 us; the launch traced here: 203 us
  blocking collectives  152 us (74%)
  starting transfers between devices  15.8 us (8%)
  Pallas kernels  12.4 us (6%)
  local copies, waits for them, and re-layouts  11.2 us (5%)
  waiting for transfers between devices  10.2 us (5%)
    all_to_all x5, blocking collectives, exchange(): return lax.all_to_all(value, axes, 0, 0, tiled=True)  152 us
    ppermute x1, starting transfers between devices, on_device(): other = lax.ppermute(mine, 'core', [(0, 1), (1, 0)])  11.5 us
    unnamed x25, local copies, waits for them, and re-layouts  11.1 us
    all_to_all x1, waiting for transfers between devices, exchange(): return lax.all_to_all(value, axes, 0, 0, tiled=True)  9.31 us
    all_to_all x1, starting transfers between devices, exchange(): return lax.all_to_all(value, axes, 0, 0, tiled=True)  4.33 us
  transfers between devices with their start and end apart: 2, of which 2 were waited for; matrix products, arithmetic and copies ran while one was open for 0% of the time, Pallas kernels for 2%

profile of v2, /device:TPU:1, one launch (start us, length us, event | category | flops | bytes accessed | tf_op | source)
XLA Modules:
  0.0 202.7 jit_solution(14399766988369114738)
XLA Ops:
  0.6 0.8 subtract_convert_fusion
  1.5 38.4 %all_to_all.30 = bf16[16,64,256]{2,1,0:T(8,128)(2,1)S(1)} all-to-all(bf16[16,64,256]{2,1,0:T(8,128)(2,1)S(1)} %broadcast_in_dim.2), channel_id=1, replica_groups=mesh['z'=16,'y'=4,'x'=4,'core'=2] {'z'}, dimensions={0} | all-to-all | bytes 1048576 | tf_op jit(solution)/shard_map/all_to_all | solution.py:232
  39.9 0.1 shard_map.112
  40.0 0.0 copy-start
  40.0 1.3 copy-done
  41.4 0.0 copy-start.11
  41.4 0.0 copy-start.7
  41.4 0.0 copy-start.9
  41.4 0.0 copy-start.10
  41.4 4.3 %all-to-all-start.1 = ((bf16[4,1024,256]{2,1,0:T(8,128)(2,1)}), bf16[4,1024,256]{2,1,0:T(8,128)(2,1)S(1)}, u32[]{:S(2)}, u32[]{:S(2)}) async-start(bf16[4,1024,256]{2,1,0:T(8,128)(2,1)} %copy-done), calls=%async_computation.1 | async-start | bytes 4194304 | tf_op jit(solution)/shard_map/all_to_all | solution.py:232
  45.7 0.0 copy-done.11
  45.7 0.1 copy.13.count_ref.counts_ref
  45.8 0.0 copy-done.7
  45.8 0.0 copy-done.9
  45.8 0.0 copy-done.10
  45.8 0.0 copy-start.1
  45.8 1.6 copy-done.1
  47.4 0.0 copy-start.2
  47.4 1.6 copy-done.2
  49.0 3.3 %shard_map.111 = (bf16[256,4096]{1,0:T(8,128)(2,1)S(1)}, bf16[4096,256]{1,0:T(8,128)(2,1)S(1)}, bf16[256,2048]{1,0:T(8,128)(2,1)S(1)}, f32[256,1]{1,0:T(8,128)S(...) custom-call(s32[64,8]{1,0:T(8,128)S(1)} %copy.13.count_ref.counts_ref, bf16[4096,256]{1,0:T(8,128)(2,1)S(1)} %copy-done.1, ...), custom_call_target="tpu_custom_call" | custom-call | flops 16777216 | bytes 9437184 | tf_op jit(solution)/shard_map/pallas_call | solution.py:251
  52.3 0.0 copy-start.3
  52.3 1.3 copy-done.3
  53.6 0.0 copy-start.5
  53.6 1.4 copy-done.5
  55.0 9.3 %all-to-all-done.1 = bf16[4,1024,256]{2,1,0:T(8,128)(2,1)S(1)} async-done(((bf16[4,1024,256]{2,1,0:T(8,128)(2,1)}), bf16[4,1024,256]{2,1,0:T(8,128)(2,1)S(1)}, u32[]{:S(2)}, u32[]{:S(2)}) %all-to-all-start.1) | async-done | bytes 2097184 | tf_op jit(solution)/shard_map/all_to_all | solution.py:232
  64.3 0.0 copy-start.4
  64.3 1.6 copy-done.4
  65.9 0.0 copy-start.6
  65.9 1.6 copy-done.6
  67.5 2.4 %shard_map.113 = bf16[4096,256]{1,0:T(8,128)(2,1)S(1)} custom-call(bf16[256,4096]{1,0:T(8,128)(2,1)S(1)} %copy-done.4, bf16[4096,256]{1,0:T(8,128)(2,1)S(1)} %bitcast.10, f32[256,1]{1,0:T(8,128)S(1)} %get-tuple-element.15.bias_ref, f32[256,1]{1,0:T(8,128)S(1)} %get-tuple-element.16.alive_ref, bf16[4096,256]{1,0:T(8,128)(2,1)S(1)} %copy-done.6), custom_call_target="tpu_custom_call" | custom-call | flops 1073741824 | bytes 8388608 | tf_op jit(solution)/shard_map/pallas_call | solution.py:273
  69.9 20.1 %all_to_all.31.in_ref = bf16[4,1024,256]{2,1,0:T(8,128)(2,1)S(1)} all-to-all(bf16[4,1024,256]{2,1,0:T(8,128)(2,1)S(1)} %bitcast.13), channel_id=1, replica_groups=mesh['z'=16,'y'=4,'x'=4,'core'=2] {'y'}, dimensions={0} | all-to-all | bytes 4194304 | tf_op jit(solution)/shard_map/all_to_all | solution.py:232
  90.0 0.3 shard_map.114
  90.3 47.5 %all_to_all.32.part_ref = bf16[16,64,256]{2,1,0:T(8,128)(2,1)S(1)} all-to-all(bf16[16,64,256]{2,1,0:T(8,128)(2,1)S(1)} %bitcast.15), channel_id=1, replica_groups=mesh['z'=16,'y'=4,'x'=4,'core'=2] {'z'}, dimensions={0} | all-to-all | bytes 1048576 | tf_op jit(solution)/shard_map/all_to_all | solution.py:232
  137.7 1.0 shard_map.115
  138.8 26.2 %all_to_all.33.in_ref = bf16[16,80,128]{2,1,0:T(8,128)(2,1)S(1)} all-to-all(bf16[16,80,128]{2,1,0:T(8,128)(2,1)S(1)} %shard_map.115), channel_id=1, replica_groups=mesh['z'=16,'y'=4,'x'=4,'core'=2] {'z'}, dimensions={0} | all-to-all | bytes 655360 | tf_op jit(solution)/shard_map/all_to_all | solution.py:232
  164.9 0.3 shard_map.116
  165.2 19.4 %all_to_all.34.in_ref = bf16[16,48,1024]{2,1,0:T(8,128)(2,1)S(1)} all-to-all(bf16[16,48,1024]{2,1,0:T(8,128)(2,1)S(1)} %shard_map.116), channel_id=1, replica_groups=mesh['z'=16,'y'=4,'x'=4,'core'=2] {'y','x'}, dimensions={0} | all-to-all | bytes 3145728 | tf_op jit(solution)/shard_map/all_to_all | solution.py:232
  184.6 2.6 %shard_map.117 = (bf16[128,4096]{1,0:T(8,128)(2,1)S(1)}, bf16[32,4096]{1,0:T(8,128)(2,1)}, bf16[32,4096]{1,0:T(8,128)(2,1)}, f32[1,256]{1,0:T(1,128)}) custom-call(s32[64,8]{1,0:T(8,128)S(1)} %copy.13.count_ref.counts_ref, s32[64,8]{1,0:T(8,128)S(1)} %copy.13.count_ref.counts_ref, bf16[16,48,1024]{2,1,0:T(8,128)(2,1)S(1)} %all_to_all.34.in_ref), custom_call_target="tpu_custom_call" | custom-call | flops 4194304 | bytes 4194304 | tf_op jit(solution)/shard_map/pallas_call | solution.py:291
  187.2 11.5 %collective-permute-start = (bf16[128,4096]{1,0:T(8,128)(2,1)S(1)}, bf16[128,4096]{1,0:T(8,128)(2,1)S(1)}, u32[]{:S(2)}, u32[]{:S(2)}) collective-permute-start(bf16[128,4096]{1,0:T(8,128)(2,1)S(1)} %get-tuple-element.22.mine_ref), channel_id=1, source_target_pairs={{0,1},{1,0},{2,3},{3,2},{4,5},{5,4},{6,7},{7,6},{8,9},{9,8},{10,11... | collective-permute-start | bytes 3145736 | tf_op jit(solution)/shard_map/ppermute | solution.py:304
  198.7 0.0 copy-start.8
  198.7 0.7 copy-done.8
  199.4 0.7 shard_map.118.tokens_ref
  200.0 0.9 collective-permute-done.other_ref
  201.0 1.7 shard_map.119
  (1 shorter events, 0.0 us)
Async XLA Ops:
  40.0 1.3 copy-start
  41.4 4.3 %copy-start.11 = (s32[64,8]{0,1:T(8,128)S(1)}, s32[64,8]{0,1:T(8,128)}, u32[]{:S(2)}) copy-start(s32[64,8]{0,1:T(8,128)} %param.14) | copy-start | bytes 6148
  41.4 4.4 %copy-start.7 = (s32[64,1,32]{0,2,1:T(8,128)S(1)}, s32[64,1,32]{0,2,1:T(8,128)}, u32[]{:S(2)}) copy-start(s32[64,1,32]{0,2,1:T(8,128)} %param.15) | copy-start | bytes 24580
  41.4 4.4 %copy-start.9 = (f32[256]{0:T(256)S(1)}, f32[256]{0:T(256)}, u32[]{:S(2)}) copy-start(f32[256]{0:T(256)} %param.11) | copy-start | bytes 3076
  41.4 4.4 %copy-start.10 = (s32[1,256]{1,0:T(1,128)S(1)}, s32[1,256]{1,0:T(1,128)}, u32[]{:S(2)}) copy-start(s32[1,256]{1,0:T(1,128)} %dead_ref.1) | copy-start | bytes 3076
  41.4 22.9 %all-to-all-start.1 = ((bf16[4,1024,256]{2,1,0:T(8,128)(2,1)}), bf16[4,1024,256]{2,1,0:T(8,128)(2,1)S(1)}, u32[]{:S(2)}, u32[]{:S(2)}) async-start(bf16[4,1024,256]{2,1,0:T(8,128)(2,1)} %copy-done), calls=%async_computation.1 | async-start | bytes 4194304 | tf_op jit(solution)/shard_map/all_to_all | solution.py:232
  45.8 1.6 copy-start.1
  47.4 1.6 copy-start.2
  52.3 1.3 copy-start.3
  53.6 1.4 copy-start.5
  64.3 1.6 copy-start.4
  65.9 1.6 copy-start.6
  187.2 13.8 %collective-permute-start = (bf16[128,4096]{1,0:T(8,128)(2,1)S(1)}, bf16[128,4096]{1,0:T(8,128)(2,1)S(1)}, u32[]{:S(2)}, u32[]{:S(2)}) collective-permute-start(bf16[128,4096]{1,0:T(8,128)(2,1)S(1)} %get-tuple-element.22.mine_ref), channel_id=1, source_target_pairs={{0,1},{1,0},{2,3},{3,2},{4,5},{5,4},{6,7},{7,6},{8,9},{9,8},{10,11... | collective-permute-start | bytes 3145736 | tf_op jit(solution)/shard_map/ppermute | solution.py:304
  198.7 0.7 copy-start.8

commit v3 on v2

v3 whole, which is shorter than its diff:
```python
import jax
import jax.numpy as jnp
from jax import lax
from jax.experimental import pallas as pl
from jax.experimental.pallas import tpu as pltpu
from jax.sharding import Mesh, PartitionSpec as P

ENC_GAIN = 0.2
EPSILON = 1e-06
F32 = jnp.float32
BF16 = jnp.bfloat16
VM = pl.BlockSpec(memory_space=pltpu.VMEM)
SM = pl.BlockSpec(memory_space=pltpu.SMEM)
EXTRA = 16


def kernel_call(body, out_shape, in_specs, flops, mib, scratch=(), out_specs=None):
    multi = isinstance(out_shape, (tuple, list))
    if out_specs is None:
        out_specs = [VM] * len(out_shape) if multi else VM
    return pl.pallas_call(
        body,
        out_shape=out_shape,
        in_specs=in_specs,
        out_specs=out_specs,
        scratch_shapes=list(scratch),
        compiler_params=pltpu.CompilerParams(vmem_limit_bytes=(mib + 4) << 20),
        cost_estimate=pl.CostEstimate(
            flops=flops, bytes_accessed=mib << 20, transcendentals=0
        ),
    )


def split3(v):
    hi = v.astype(BF16)
    rest = v - hi.astype(F32)
    mid = rest.astype(BF16)
    lo = (rest - mid.astype(F32)).astype(BF16)
    return hi, mid, lo


def spread(in_ref, out_ref):
    for y in range(4):
        out_ref[y] = in_ref[...]


def forward(count_ref, g_ref, enc_ref, dec_ref, bias_ref, dead_ref, out_ref, t_ref, stat_ref):
    latents = enc_ref.shape[1]
    feat = lax.axis_index("z") * 4 + lax.axis_index("y")
    row = lax.broadcasted_iota(jnp.int32, (latents, latents), 0)
    col = lax.broadcasted_iota(jnp.int32, (latents, latents), 1)
    slot = lax.broadcasted_iota(jnp.int32, (latents, 1), 0)
    limit = jnp.zeros((latents, 1), jnp.int32)
    for t in range(8):
        limit = jnp.where(slot // 32 == t, count_ref[t, feat], limit)
    dead = jnp.sum(jnp.where(row == col, dead_ref[...], 0), axis=1, keepdims=True)
    dead = jnp.where(slot % 32 < limit, dead, -1)
    alive = 1.0 - jnp.max(jnp.where(dead == col, 1.0, 0.0), axis=0, keepdims=True)

    total = jnp.zeros((1, latents), F32)
    pre = bias_ref[...]
    for z in range(16):
        for pair in range(2):
            y = 2 * pair
            both = jnp.concatenate(
                [
                    g_ref[pl.ds((y * 16 + z) * 64, 64), :],
                    g_ref[pl.ds(((y + 1) * 16 + z) * 64, 64), :],
                ],
                0,
            )
            t_ref[:, pl.ds(z * 256 + pair * 128, 128)] = both.T
        rows = enc_ref[pl.ds(z * 256, 256), :]
        wide = rows.astype(F32)
        total = total + jnp.sum(wide * wide, axis=0, keepdims=True)
        pre = pre + jnp.dot(t_ref[:, pl.ds(z * 256, 256)], rows, preferred_element_type=F32)
    stat_ref[...] = jnp.sum(jnp.sqrt(total) * alive, axis=1, keepdims=True)
    feat = (jnp.maximum(pre, 0.0) * alive).astype(BF16)
    for y in range(4):
        for part in range(4):
            out_ref[y, :, pl.ds(part * 256, 256)] = jnp.dot(
                feat,
                dec_ref[:, pl.ds(y * 1024 + part * 256, 256)],
                preferred_element_type=F32,
            ).astype(BF16)


def fold(in_ref, out_ref):
    for block in range(8):
        cols = pl.ds(block * 128, 128)
        total = in_ref[0, :, cols].astype(F32)
        for y in range(1, 4):
            total = total + in_ref[y, :, cols].astype(F32)
        out_ref[cols, :] = total.astype(BF16).T


def residual(part_ref, g_ref, sample_ref, stat_ref, out_ref):
    source = lax.axis_index("y") * 16 + lax.axis_index("z")
    own = g_ref[(source % 4) * 16 + source // 4]
    recon = part_ref[0].astype(F32)
    for z in range(1, 16):
        recon = recon + part_ref[z].astype(F32)
    error = own.astype(F32) - recon
    loss = jnp.sum(error * error, axis=0, keepdims=True)
    loss = jnp.concatenate([loss[:, :128], loss[:, 128:]], 0)
    stat = jnp.broadcast_to(stat_ref[...], (2, 128))
    pad = jnp.zeros((4, 128), F32)
    pieces = [split3(v) for v in (loss, stat)]
    extra = jnp.concatenate([p.astype(F32) for s in pieces for p in s] + [pad], 0).astype(BF16)
    error_b = error.astype(BF16)
    sample = sample_ref[...]
    shard = lax.broadcasted_iota(jnp.int32, sample.shape, 1)
    wide = jnp.concatenate([jnp.where(shard % 4 == y, sample, 0) for y in range(4)], 0)
    wide = jnp.concatenate([wide, jnp.zeros_like(wide)], 1).T
    token = lax.broadcasted_iota(jnp.int32, (error.shape[1], 128), 0)
    for z in range(16):
        wanted = jnp.sum(wide[z * 4 : z * 4 + 4], axis=0, keepdims=True)
        onehot = jnp.where(token == wanted, 1.0, 0.0).astype(BF16)
        picked = jnp.dot(error_b, onehot, preferred_element_type=F32)
        out_ref[z, pl.ds(0, 64), :] = picked.astype(BF16)
        out_ref[z, pl.ds(64, EXTRA), :] = extra


def relay(in_ref, out_ref):
    riders = in_ref[0, pl.ds(64, EXTRA), :].astype(F32)
    hi, mid, lo = riders[0:2], riders[2:4], riders[4:6]
    shi, smid, slo = riders[6:8], riders[8:10], riders[10:12]
    loss = hi + mid + lo
    stat = shi + smid + slo
    for z in range(1, 16):
        riders = in_ref[z, pl.ds(64, EXTRA), :].astype(F32)
        loss = loss + (riders[0:2] + riders[2:4] + riders[4:6])
        stat = stat + (riders[6:8] + riders[8:10] + riders[10:12])
    row = jnp.concatenate([loss[0:1], loss[1:2], stat[0:1]], 1)
    row = jnp.concatenate(
        [p.astype(F32) for p in split3(row)] + [jnp.zeros((EXTRA - 3, 384), F32)], 0
    ).astype(BF16)
    row = jnp.concatenate([row, jnp.zeros((EXTRA, 640), BF16)], 1)
    for pair in range(8):
        both = jnp.concatenate(
            [in_ref[2 * pair, pl.ds(0, 64), :], in_ref[2 * pair + 1, pl.ds(0, 64), :]], 0
        ).T
        for y in range(4):
            for x in range(4):
                out_ref[y * 4 + x, pl.ds(0, 32), pl.ds(pair * 128, 128)] = both[
                    y * 32 : y * 32 + 32
                ]
    for block in range(16):
        out_ref[block, pl.ds(32, EXTRA), :] = row


def tile_scale(in_ref, count, x):
    squares = jnp.zeros((32, 1024), F32)
    for y in range(4):
        rows = in_ref[y * 4 + x, pl.ds(0, 32), :].astype(F32)
        squares = squares + rows * rows
    squares = jnp.sum(squares, axis=1, keepdims=True)
    slot = lax.broadcasted_iota(jnp.int32, (32, 1), 0)
    return lax.rsqrt(squares + EPSILON) * jnp.where(slot < count, 1.0, 0.0)


def read_riders(counts_ref, in_ref, x):
    riders = jnp.zeros((EXTRA, 384), F32)
    for y in range(4):
        riders = riders + in_ref[y * 4 + x, pl.ds(32, EXTRA), pl.ds(0, 384)].astype(F32)
    riders = riders[0:1] + riders[1:2] + riders[2:3]
    dead = jnp.sum(counts_ref[...].astype(F32), axis=0, keepdims=True)
    dead = jnp.sum(dead, axis=1, keepdims=True)
    gain = ENC_GAIN * (riders[:, 256:257] / (16384.0 - dead))
    return riders[:, :256], gain


def normalise(count_ref, counts_ref, in_ref, rows_ref):
    feat = lax.axis_index("z") * 4 + lax.axis_index("y")
    core = lax.axis_index("core")
    _, gain = read_riders(counts_ref, in_ref, 0)
    for x in range(4):
        scale = tile_scale(in_ref, count_ref[x * 2 + core, feat], x)
        for y in range(4):
            unit = in_ref[y * 4 + x, pl.ds(0, 32), :].astype(F32) * scale
            rows_ref[pl.ds(x * 32, 32), pl.ds(y * 1024, 1024)] = (gain * unit).astype(BF16)


def finish(count_ref, counts_ref, in_ref, rows_ref, t_ref, enc_ref, dec_ref, loss_ref, half_ref):
    feat = lax.axis_index("z") * 4 + lax.axis_index("y")
    x_own = lax.axis_index("x")
    core = lax.axis_index("core")
    loss, _ = read_riders(counts_ref, in_ref, x_own)
    loss_ref[...] = loss * (1.0 / 4096.0)
    for x in range(4):

        @pl.when(x == x_own)
        def _(x=x):
            scale = tile_scale(in_ref, count_ref[x * 2 + core, feat], x)
            for y in range(4):
                cols = pl.ds(y * 1024, 1024)
                unit = in_ref[y * 4 + x, pl.ds(0, 32), :].astype(F32) * scale
                dec_ref[:, cols] = unit.astype(BF16)
            enc_ref[...] = rows_ref[pl.ds(x * 32, 32), :]

    half_ref[...] = lax.dot_general(
        t_ref[...], rows_ref[...], (((1,), (1,)), ((), ())), preferred_element_type=F32
    )


def reencode(rows_ref, t_ref, half_ref, out_ref):
    core = lax.axis_index("core")
    other = lax.dot_general(
        t_ref[...], rows_ref[...], (((1,), (1,)), ((), ())), preferred_element_type=F32
    )
    own = half_ref[...]
    first = jnp.where(core == 0, own, other)
    second = jnp.where(core == 0, other, own)
    slots = []
    for x in range(4):
        slots += [first[:, x * 32 : x * 32 + 32], second[:, x * 32 : x * 32 + 32]]
    out_ref[...] = jnp.maximum(jnp.concatenate(slots, 1), 0.0).astype(BF16)


def exchange(value, axes):
    return lax.all_to_all(value, axes, 0, 0, tiled=True)


def shape(*dims, dtype=BF16):
    return jax.ShapeDtypeStruct(dims, dtype)


def on_device(acts, dec_bias, enc_weight, enc_bias, dec_weight, dead_ids, tile_count, sample_rows):
    width, latents = enc_weight.shape
    depth, tokens = acts.shape
    tile = sample_rows.shape[2]
    slots = dead_ids.shape[1]

    counts = tile_count.T
    centered = (acts.astype(F32) - dec_bias[:, None]).astype(BF16)
    by_z = lax.all_gather(centered, "z", axis=0, tiled=True)
    by_z = kernel_call(spread, shape(4, 16 * depth, tokens), [VM], 1 << 20, 3)(by_z)
    gathered = exchange(by_z, "y").reshape(width, tokens)

    recon, by_token, stat = kernel_call(
        forward,
        (shape(4, tokens, width // 4), shape(tokens, width), shape(1, 1, dtype=F32)),
        [SM] + [VM] * 5,
        4 * width * latents * tokens,
        10,
    )(counts, gathered, enc_weight, dec_weight, enc_bias.reshape(1, latents), dead_ids)

    part = exchange(recon, "y")
    part = kernel_call(fold, shape(width // 4, tokens), [VM], 1 << 20, 3)(part)
    part = exchange(part.reshape(16, depth, tokens), "z")

    picks = kernel_call(
        residual,
        shape(16, depth + EXTRA, 4 * tile),
        [VM] * 4,
        2 * depth * tokens * 64 * tile,
        4,
    )(
        part,
        gathered.reshape(64, depth, tokens),
        sample_rows.transpose(1, 2, 0).reshape(tile, 64),
        stat,
    )
    picks = exchange(picks, "z")
    picks = kernel_call(relay, shape(16, tile + EXTRA, width // 4), [VM], 1 << 20, 2)(picks)
    picks = exchange(picks, ("y", "x"))
    rows = kernel_call(normalise, shape(4 * tile, width), [SM, VM, VM], 1 << 21, 3)(
        counts, counts, picks
    )
    other = lax.ppermute(rows, "core", [(0, 1), (1, 0)])
    new_enc, new_dec, token_loss, half = kernel_call(
        finish,
        (
            shape(tile, width),
            shape(tile, width),
            shape(1, tokens, dtype=F32),
            shape(tokens, 4 * tile, dtype=F32),
        ),
        [SM] + [VM] * 4,
        tokens * slots * width,
        6,
    )(counts, counts, picks, rows, by_token)
    reencoded = kernel_call(
        reencode, shape(tokens, slots), [VM] * 3, tokens * slots * width, 4
    )(other, by_token, half)
    return (new_enc, new_dec, reencoded, token_loss.reshape(tokens))


def solution(mesh):
    fine = Mesh(mesh.devices.reshape(16, 4, 4, 2), ("z", "y", "x", "core"))
    feat, tok = ("z", "y"), ("x", "core")
    in_specs = (
        P(feat, tok),
        P(feat),
        P(None, feat),
        P(feat),
        P(feat, None),
        P(feat, None),
        P(),
        P(None, tok, None),
    )
    out_specs = (P(feat + tok, None), P(feat + tok, None), P(tok, feat), P(tok))
    return jax.shard_map(
        on_device, mesh=fine, in_specs=in_specs, out_specs=out_specs, check_vma=False
    )
```

time: 206 us -> 167 us (0.81); the launches traced: 203 us -> 166 us
  local copies, waits for them, and re-layouts: 11.2 us -> 0.03 us
  blocking collectives: 152 us -> 142 us
  waiting for transfers between devices: 10.2 us -> 0.65 us
  Pallas kernels: 12.4 us -> 9.16 us
  starting transfers between devices: 15.8 us -> 12.8 us
    all_to_all x5, blocking collectives: 152 us -> 110 us  [exchange(): return lax.all_to_all(value, axes, 0, 0, tiled=True)]
    all_gather x0 -> x1, blocking collectives: none -> 31.8 us  [on_device(): by_z = lax.all_gather(centered, 'z', axis=0, tiled=True)]
    unnamed x25 -> x12, local copies, waits for them, and re-layouts: 11.1 us -> 0.03 us
    all_to_all x1 -> x0, waiting for transfers between devices: 9.31 us -> none  [exchange(): return lax.all_to_all(value, axes, 0, 0, tiled=True)]
    all_to_all x1 -> x0, starting transfers between devices: 4.33 us -> none  [exchange(): return lax.all_to_all(value, axes, 0, 0, tiled=True)]
    pallas_call x5 -> x4, Pallas kernels: 10.7 us -> 7.25 us  [the longest x1 3.1 us: on_device(): kernel_call(forward, (shape(4, tokens, width // 4), shape(tokens, width),...]
  transfers between devices with their start and end apart: 2 -> 1, of which waited for: 2 -> 1; matrix products, arithmetic and copies ran while one was open for 0% -> 0% of each run, Pallas kernels for 2% -> 1%
where the time goes in v3:
time: 167 us; the launch traced here: 166 us
  blocking collectives  142 us (85%)
  starting transfers between devices  12.8 us (8%)
  Pallas kernels  9.16 us (5%)
    all_to_all x5, blocking collectives, exchange(): return lax.all_to_all(value, axes, 0, 0, tiled=True)  110 us
    all_gather x1, blocking collectives, on_device(): by_z = lax.all_gather(centered, 'z', axis=0, tiled=True)  31.8 us
    ppermute x1, starting transfers between devices, on_device(): other = lax.ppermute(rows, 'core', [(0, 1), (1, 0)])  12.8 us
  transfers between devices with their start and end apart: 1, of which 1 were waited for; matrix products, arithmetic and copies ran while one was open for 0% of the time, Pallas kernels for 1%

profile of v3, /device:TPU:1, one launch (start us, length us, event | category | flops | bytes accessed | tf_op | source)
XLA Modules:
  0.0 166.1 jit_solution(12583616433909583660)
XLA Ops:
  0.6 0.8 subtract_convert_fusion
  1.5 31.8 %all_gather.3.in_ref = bf16[1024,256]{1,0:T(8,128)(2,1)S(1)} all-gather(bf16[64,256]{1,0:T(8,128)(2,1)S(1)} %subtract_convert_fusion), channel_id=1, replica_groups=mesh['z'=16,'y'=4,'x'=4,'core'=2] {'z'}, dimensions={0}, use_global_device_ids=true | all-gather | bytes 557056 | tf_op jit(solution)/shard_map/all_gather | solution.py:236
  33.3 0.0 copy-start.5
  33.3 0.1 shard_map.111
  33.4 0.0 copy-start
  33.4 0.0 copy-start.1
  33.4 0.0 copy-start.2
  33.5 0.0 copy-start.4
  33.5 21.9 %all_to_all.25 = bf16[4,1024,256]{2,1,0:T(8,128)(2,1)S(1)} all-to-all(bf16[4,1024,256]{2,1,0:T(8,128)(2,1)S(1)} %shard_map.111), channel_id=1, replica_groups=mesh['z'=16,'y'=4,'x'=4,'core'=2] {'y'}, dimensions={0} | all-to-all | bytes 4194304 | tf_op jit(solution)/shard_map/all_to_all | solution.py:221
  55.4 0.0 copy-done.5
  55.4 0.0 copy-done
  55.4 0.0 copy-done.1
  55.4 0.0 copy-done.2
  55.4 0.0 copy-done.4
  55.4 3.1 %shard_map.112 = (bf16[4,256,1024]{2,1,0:T(8,128)(2,1)S(1)}, bf16[256,4096]{1,0:T(8,128)(2,1)S(1)}, f32[1,1]{1,0:T(1,128)}) custom-call(s32[8,64]{1,0:T(8,128)S(1)} %bitcast.12, bf16[4096,256]{1,0:T(8,128)(2,1)S(1)} %bitcast.9, bf16[4096,256]{1,0:T(8,128)(2,1)S(1)} %copy-done, bf16[256,4096]{1,0:T(8,128)(2,1)S(1)} %copy-done.1, f32[1,256]{1,0:T(1,128)S(1)} %bitcast.18, ...), custom_call_target="tpu_custom_call" | custom-call | flops 1073741824 | bytes 10485760 | tf_op jit(solution)/shard_map/pallas_call | solution.py:240
  58.5 19.2 %all_to_all.26.in_ref = bf16[4,256,1024]{2,1,0:T(8,128)(2,1)S(1)} all-to-all(bf16[4,256,1024]{2,1,0:T(8,128)(2,1)S(1)} %get-tuple-element.11), channel_id=1, replica_groups=mesh['z'=16,'y'=4,'x'=4,'core'=2] {'y'}, dimensions={0} | all-to-all | bytes 4194304 | tf_op jit(solution)/shard_map/all_to_all | solution.py:221
  77.7 0.0 copy-start.3
  77.7 0.4 shard_map.113
  78.2 25.2 %all_to_all.27.part_ref = bf16[16,64,256]{2,1,0:T(8,128)(2,1)S(1)} all-to-all(bf16[16,64,256]{2,1,0:T(8,128)(2,1)S(1)} %bitcast.11), channel_id=1, replica_groups=mesh['z'=16,'y'=4,'x'=4,'core'=2] {'z'}, dimensions={0} | all-to-all | bytes 1048576 | tf_op jit(solution)/shard_map/all_to_all | solution.py:221
  103.4 0.0 copy-done.3
  103.4 1.1 shard_map.114
  104.5 24.5 %all_to_all.28.in_ref = bf16[16,80,128]{2,1,0:T(8,128)(2,1)S(1)} all-to-all(bf16[16,80,128]{2,1,0:T(8,128)(2,1)S(1)} %shard_map.114), channel_id=1, replica_groups=mesh['z'=16,'y'=4,'x'=4,'core'=2] {'z'}, dimensions={0} | all-to-all | bytes 655360 | tf_op jit(solution)/shard_map/all_to_all | solution.py:221
  128.9 0.3 shard_map.115
  129.2 19.3 %all_to_all.29.in_ref = bf16[16,48,1024]{2,1,0:T(8,128)(2,1)S(1)} all-to-all(bf16[16,48,1024]{2,1,0:T(8,128)(2,1)S(1)} %shard_map.115), channel_id=1, replica_groups=mesh['z'=16,'y'=4,'x'=4,'core'=2] {'y','x'}, dimensions={0} | all-to-all | bytes 3145728 | tf_op jit(solution)/shard_map/all_to_all | solution.py:221
  148.5 1.1 shard_map.116.rows_ref
  149.6 12.8 %collective-permute-start = (bf16[128,4096]{1,0:T(8,128)(2,1)S(1)}, bf16[128,4096]{1,0:T(8,128)(2,1)S(1)}, u32[]{:S(2)}, u32[]{:S(2)}) collective-permute-start(bf16[128,4096]{1,0:T(8,128)(2,1)S(1)} %shard_map.116.rows_ref), channel_id=1, source_target_pairs={{0,1},{1,0},{2,3},{3,2},{4,5},{5,4},{6,7},{7,6},{8,9},{9,8},{10,11... | collective-permute-start | bytes 3145736 | tf_op jit(solution)/shard_map/ppermute | solution.py:270
  162.4 1.6 shard_map.117
  164.0 0.6 collective-permute-done.rows_ref
  164.7 1.5 shard_map.118
Async XLA Ops:
  33.3 22.1 %copy-start.5 = (s32[1,256]{1,0:T(1,128)S(1)}, s32[1,256]{1,0:T(1,128)}, u32[]{:S(2)}) copy-start(s32[1,256]{1,0:T(1,128)} %dead_ref.1) | copy-start | bytes 3076
  33.4 22.0 %copy-start = (bf16[4096,256]{1,0:T(8,128)(2,1)S(1)}, bf16[4096,256]{1,0:T(8,128)(2,1)}, u32[]{:S(2)}) copy-start(bf16[4096,256]{1,0:T(8,128)(2,1)} %enc_ref.1) | copy-start | bytes 6291460
  33.4 22.0 %copy-start.1 = (bf16[256,4096]{1,0:T(8,128)(2,1)S(1)}, bf16[256,4096]{1,0:T(8,128)(2,1)}, u32[]{:S(2)}) copy-start(bf16[256,4096]{1,0:T(8,128)(2,1)} %dec_ref.1) | copy-start | bytes 6291460
  33.4 22.0 %copy-start.2 = (s32[64,8]{0,1:T(8,128)S(1)}, s32[64,8]{0,1:T(8,128)}, u32[]{:S(2)}) copy-start(s32[64,8]{0,1:T(8,128)} %param.14) | copy-start | bytes 6148
  33.5 22.0 %copy-start.4 = (f32[256]{0:T(256)S(1)}, f32[256]{0:T(256)}, u32[]{:S(2)}) copy-start(f32[256]{0:T(256)} %param.11) | copy-start | bytes 3076
  77.7 25.6 %copy-start.3 = (s32[64,1,32]{0,2,1:T(8,128)S(1)}, s32[64,1,32]{0,2,1:T(8,128)}, u32[]{:S(2)}) copy-start(s32[64,1,32]{0,2,1:T(8,128)} %param.15) | copy-start | bytes 24580
  149.6 15.1 %collective-permute-start = (bf16[128,4096]{1,0:T(8,128)(2,1)S(1)}, bf16[128,4096]{1,0:T(8,128)(2,1)S(1)}, u32[]{:S(2)}, u32[]{:S(2)}) collective-permute-start(bf16[128,4096]{1,0:T(8,128)(2,1)S(1)} %shard_map.116.rows_ref), channel_id=1, source_target_pairs={{0,1},{1,0},{2,3},{3,2},{4,5},{5,4},{6,7},{7,6},{8,9},{9,8},{10,11... | collective-permute-start | bytes 3145736 | tf_op jit(solution)/shard_map/ppermute | solution.py:270

commit v4 on v3

--- a/solution.py
+++ b/solution.py
@@ -57,8 +57,6 @@
     dead = jnp.where(slot % 32 < limit, dead, -1)
     alive = 1.0 - jnp.max(jnp.where(dead == col, 1.0, 0.0), axis=0, keepdims=True)
 
-    total = jnp.zeros((1, latents), F32)
-    pre = bias_ref[...]
     for z in range(16):
         for pair in range(2):
             y = 2 * pair
@@ -70,19 +68,18 @@
                 0,
             )
             t_ref[:, pl.ds(z * 256 + pair * 128, 128)] = both.T
-        rows = enc_ref[pl.ds(z * 256, 256), :]
-        wide = rows.astype(F32)
-        total = total + jnp.sum(wide * wide, axis=0, keepdims=True)
-        pre = pre + jnp.dot(t_ref[:, pl.ds(z * 256, 256)], rows, preferred_element_type=F32)
-    stat_ref[...] = jnp.sum(jnp.sqrt(total) * alive, axis=1, keepdims=True)
+    pre = jnp.dot(t_ref[...], enc_ref[...], preferred_element_type=F32) + bias_ref[...]
     feat = (jnp.maximum(pre, 0.0) * alive).astype(BF16)
     for y in range(4):
-        for part in range(4):
-            out_ref[y, :, pl.ds(part * 256, 256)] = jnp.dot(
-                feat,
-                dec_ref[:, pl.ds(y * 1024 + part * 256, 256)],
-                preferred_element_type=F32,
-            ).astype(BF16)
+        out_ref[y] = jnp.dot(
+            feat, dec_ref[:, pl.ds(y * 1024, 1024)], preferred_element_type=F32
+        ).astype(BF16)
+    total = jnp.zeros((8, latents), F32)
+    for part in range(16):
+        wide = enc_ref[pl.ds(part * 256, 256), :].astype(F32)
+        total = total + jnp.sum((wide * wide).reshape(32, 8, latents), axis=0)
+    norms = jnp.sqrt(jnp.sum(total, axis=0, keepdims=True))
+    stat_ref[...] = jnp.sum(norms * alive, axis=1, keepdims=True)
 
 
 def fold(in_ref, out_ref):
@@ -131,28 +128,23 @@
         riders = in_ref[z, pl.ds(64, EXTRA), :].astype(F32)
         loss = loss + (riders[0:2] + riders[2:4] + riders[4:6])
         stat = stat + (riders[6:8] + riders[8:10] + riders[10:12])
-    row = jnp.concatenate([loss[0:1], loss[1:2], stat[0:1]], 1)
-    row = jnp.concatenate(
-        [p.astype(F32) for p in split3(row)] + [jnp.zeros((EXTRA - 3, 384), F32)], 0
-    ).astype(BF16)
-    row = jnp.concatenate([row, jnp.zeros((EXTRA, 640), BF16)], 1)
+    pieces = [p.astype(F32) for v in (loss, stat) for p in split3(v)]
+    riders = jnp.concatenate(pieces + [jnp.zeros((20, 128), F32)], 0).astype(BF16)
     for pair in range(8):
         both = jnp.concatenate(
             [in_ref[2 * pair, pl.ds(0, 64), :], in_ref[2 * pair + 1, pl.ds(0, 64), :]], 0
         ).T
         for y in range(4):
             for x in range(4):
-                out_ref[y * 4 + x, pl.ds(0, 32), pl.ds(pair * 128, 128)] = both[
-                    y * 32 : y * 32 + 32
-                ]
+                out_ref[y * 4 + x, :, pl.ds(pair * 128, 128)] = both[y * 32 : y * 32 + 32]
     for block in range(16):
-        out_ref[block, pl.ds(32, EXTRA), :] = row
+        out_ref[block, :, pl.ds(1024, 128)] = riders
 
 
 def tile_scale(in_ref, count, x):
     squares = jnp.zeros((32, 1024), F32)
     for y in range(4):
-        rows = in_ref[y * 4 + x, pl.ds(0, 32), :].astype(F32)
+        rows = in_ref[y * 4 + x, :, pl.ds(0, 1024)].astype(F32)
         squares = squares + rows * rows
     squares = jnp.sum(squares, axis=1, keepdims=True)
     slot = lax.broadcasted_iota(jnp.int32, (32, 1), 0)
@@ -160,14 +152,15 @@
 
 
 def read_riders(counts_ref, in_ref, x):
-    riders = jnp.zeros((EXTRA, 384), F32)
-    for y in range(4):
-        riders = riders + in_ref[y * 4 + x, pl.ds(32, EXTRA), pl.ds(0, 384)].astype(F32)
-    riders = riders[0:1] + riders[1:2] + riders[2:3]
+    riders = jnp.zeros((EXTRA, 128), F32)
+    for y in range(4):
+        riders = riders + in_ref[y * 4 + x, pl.ds(0, EXTRA), pl.ds(1024, 128)].astype(F32)
+    loss = riders[0:2] + riders[2:4] + riders[4:6]
+    stat = riders[6:7] + riders[8:9] + riders[10:11]
     dead = jnp.sum(counts_ref[...].astype(F32), axis=0, keepdims=True)
     dead = jnp.sum(dead, axis=1, keepdims=True)
-    gain = ENC_GAIN * (riders[:, 256:257] / (16384.0 - dead))
-    return riders[:, :256], gain
+    gain = ENC_GAIN * (stat[:, 0:1] / (16384.0 - dead))
+    return jnp.concatenate([loss[0:1], loss[1:2]], 1), gain
 
 
 def normalise(count_ref, counts_ref, in_ref, rows_ref):
@@ -177,7 +170,7 @@
     for x in range(4):
         scale = tile_scale(in_ref, count_ref[x * 2 + core, feat], x)
         for y in range(4):
-            unit = in_ref[y * 4 + x, pl.ds(0, 32), :].astype(F32) * scale
+            unit = in_ref[y * 4 + x, :, pl.ds(0, 1024)].astype(F32) * scale
             rows_ref[pl.ds(x * 32, 32), pl.ds(y * 1024, 1024)] = (gain * unit).astype(BF16)
 
 
@@ -194,7 +187,7 @@
             scale = tile_scale(in_ref, count_ref[x * 2 + core, feat], x)
             for y in range(4):
                 cols = pl.ds(y * 1024, 1024)
-                unit = in_ref[y * 4 + x, pl.ds(0, 32), :].astype(F32) * scale
+                unit = in_ref[y * 4 + x, :, pl.ds(0, 1024)].astype(F32) * scale
                 dec_ref[:, cols] = unit.astype(BF16)
             enc_ref[...] = rows_ref[pl.ds(x * 32, 32), :]
 
@@ -262,7 +255,7 @@
         stat,
     )
     picks = exchange(picks, "z")
-    picks = kernel_call(relay, shape(16, tile + EXTRA, width // 4), [VM], 1 << 20, 2)(picks)
+    picks = kernel_call(relay, shape(16, tile, width // 4 + 128), [VM], 1 << 20, 2)(picks)
     picks = exchange(picks, ("y", "x"))
     rows = kernel_call(normalise, shape(4 * tile, width), [SM, VM, VM], 1 << 21, 3)(
         counts, counts, picks

time: 167 us -> 164 us (0.982)
  blocking collectives: 142 us -> 140 us
    all_to_all x5, blocking collectives: 110 us -> 108 us  [exchange(): return lax.all_to_all(value, axes, 0, 0, tiled=True)]
where the time goes in v4:
time: 164 us
  blocking collectives  140 us (85%)
  starting transfers between devices  12.9 us (8%)
  Pallas kernels  9.07 us (6%)
    all_to_all x5, blocking collectives, exchange(): return lax.all_to_all(value, axes, 0, 0, tiled=True)  108 us
    all_gather x1, blocking collectives, on_device(): by_z = lax.all_gather(centered, 'z', axis=0, tiled=True)  31.8 us
    ppermute x1, starting transfers between devices, on_device(): other = lax.ppermute(rows, 'core', [(0, 1), (1, 0)])  12.9 us
  transfers between devices with their start and end apart: 1, of which 1 were waited for; matrix products, arithmetic and copies ran while one was open for 0% of the time, Pallas kernels for 1%

profile of v4, /device:TPU:1, one launch (start us, length us, event | category | flops | bytes accessed | tf_op | source)
XLA Modules:
  0.0 163.9 jit_solution(13423689278684354778)
XLA Ops:
  0.6 0.8 subtract_convert_fusion
  1.5 31.8 %all_gather.3.in_ref = bf16[1024,256]{1,0:T(8,128)(2,1)S(1)} all-gather(bf16[64,256]{1,0:T(8,128)(2,1)S(1)} %subtract_convert_fusion), channel_id=1, replica_groups=mesh['z'=16,'y'=4,'x'=4,'core'=2] {'z'}, dimensions={0}, use_global_device_ids=true | all-gather | bytes 557056 | tf_op jit(solution)/shard_map/all_gather | solution.py:229
  33.3 0.0 copy-start.5
  33.3 0.1 shard_map.111
  33.4 0.0 copy-start
  33.4 0.0 copy-start.1
  33.4 0.0 copy-start.2
  33.5 0.0 copy-start.4
  33.5 21.9 %all_to_all.25 = bf16[4,1024,256]{2,1,0:T(8,128)(2,1)S(1)} all-to-all(bf16[4,1024,256]{2,1,0:T(8,128)(2,1)S(1)} %shard_map.111), channel_id=1, replica_groups=mesh['z'=16,'y'=4,'x'=4,'core'=2] {'y'}, dimensions={0} | all-to-all | bytes 4194304 | tf_op jit(solution)/shard_map/all_to_all | solution.py:214
  55.4 0.0 copy-done.5
  55.4 0.0 copy-done
  55.4 0.0 copy-done.1
  55.4 0.0 copy-done.2
  55.4 0.0 copy-done.4
  55.4 3.1 %shard_map.112 = (bf16[4,256,1024]{2,1,0:T(8,128)(2,1)S(1)}, bf16[256,4096]{1,0:T(8,128)(2,1)S(1)}, f32[1,1]{1,0:T(1,128)}) custom-call(s32[8,64]{1,0:T(8,128)S(1)} %bitcast.12, bf16[4096,256]{1,0:T(8,128)(2,1)S(1)} %bitcast.9, bf16[4096,256]{1,0:T(8,128)(2,1)S(1)} %copy-done, bf16[256,4096]{1,0:T(8,128)(2,1)S(1)} %copy-done.1, f32[1,256]{1,0:T(1,128)S(1)} %bitcast.18, ...), custom_call_target="tpu_custom_call" | custom-call | flops 1073741824 | bytes 10485760 | tf_op jit(solution)/shard_map/pallas_call | solution.py:233
  58.5 19.2 %all_to_all.26.in_ref = bf16[4,256,1024]{2,1,0:T(8,128)(2,1)S(1)} all-to-all(bf16[4,256,1024]{2,1,0:T(8,128)(2,1)S(1)} %get-tuple-element.11), channel_id=1, replica_groups=mesh['z'=16,'y'=4,'x'=4,'core'=2] {'y'}, dimensions={0} | all-to-all | bytes 4194304 | tf_op jit(solution)/shard_map/all_to_all | solution.py:214
  77.7 0.0 copy-start.3
  77.7 0.4 shard_map.113
  78.1 25.2 %all_to_all.27.part_ref = bf16[16,64,256]{2,1,0:T(8,128)(2,1)S(1)} all-to-all(bf16[16,64,256]{2,1,0:T(8,128)(2,1)S(1)} %bitcast.11), channel_id=1, replica_groups=mesh['z'=16,'y'=4,'x'=4,'core'=2] {'z'}, dimensions={0} | all-to-all | bytes 1048576 | tf_op jit(solution)/shard_map/all_to_all | solution.py:214
  103.3 0.0 copy-done.3
  103.3 1.1 shard_map.114
  104.4 24.5 %all_to_all.28.in_ref = bf16[16,80,128]{2,1,0:T(8,128)(2,1)S(1)} all-to-all(bf16[16,80,128]{2,1,0:T(8,128)(2,1)S(1)} %shard_map.114), channel_id=1, replica_groups=mesh['z'=16,'y'=4,'x'=4,'core'=2] {'z'}, dimensions={0} | all-to-all | bytes 655360 | tf_op jit(solution)/shard_map/all_to_all | solution.py:214
  128.9 0.2 shard_map.115
  129.1 17.1 %all_to_all.29.in_ref = bf16[16,32,1152]{2,1,0:T(8,128)(2,1)S(1)} all-to-all(bf16[16,32,1152]{2,1,0:T(8,128)(2,1)S(1)} %shard_map.115), channel_id=1, replica_groups=mesh['z'=16,'y'=4,'x'=4,'core'=2] {'y','x'}, dimensions={0} | all-to-all | bytes 2359296 | tf_op jit(solution)/shard_map/all_to_all | solution.py:214
  146.2 1.1 shard_map.116.rows_ref
  147.3 12.9 %collective-permute-start = (bf16[128,4096]{1,0:T(8,128)(2,1)S(1)}, bf16[128,4096]{1,0:T(8,128)(2,1)S(1)}, u32[]{:S(2)}, u32[]{:S(2)}) collective-permute-start(bf16[128,4096]{1,0:T(8,128)(2,1)S(1)} %shard_map.116.rows_ref), channel_id=1, source_target_pairs={{0,1},{1,0},{2,3},{3,2},{4,5},{5,4},{6,7},{7,6},{8,9},{9,8},{10,11... | collective-permute-start | bytes 3145736 | tf_op jit(solution)/shard_map/ppermute | solution.py:263
  160.2 1.6 shard_map.117
  161.8 0.6 collective-permute-done.rows_ref
  162.4 1.5 shard_map.118
Async XLA Ops:
  33.3 22.1 %copy-start.5 = (s32[1,256]{1,0:T(1,128)S(1)}, s32[1,256]{1,0:T(1,128)}, u32[]{:S(2)}) copy-start(s32[1,256]{1,0:T(1,128)} %dead_ref.1) | copy-start | bytes 3076
  33.4 22.0 %copy-start = (bf16[4096,256]{1,0:T(8,128)(2,1)S(1)}, bf16[4096,256]{1,0:T(8,128)(2,1)}, u32[]{:S(2)}) copy-start(bf16[4096,256]{1,0:T(8,128)(2,1)} %enc_ref.1) | copy-start | bytes 6291460
  33.4 22.0 %copy-start.1 = (bf16[256,4096]{1,0:T(8,128)(2,1)S(1)}, bf16[256,4096]{1,0:T(8,128)(2,1)}, u32[]{:S(2)}) copy-start(bf16[256,4096]{1,0:T(8,128)(2,1)} %dec_ref.1) | copy-start | bytes 6291460
  33.4 22.0 %copy-start.2 = (s32[64,8]{0,1:T(8,128)S(1)}, s32[64,8]{0,1:T(8,128)}, u32[]{:S(2)}) copy-start(s32[64,8]{0,1:T(8,128)} %param.14) | copy-start | bytes 6148
  33.5 22.0 %copy-start.4 = (f32[256]{0:T(256)S(1)}, f32[256]{0:T(256)}, u32[]{:S(2)}) copy-start(f32[256]{0:T(256)} %param.11) | copy-start | bytes 3076
  77.7 25.6 %copy-start.3 = (s32[64,1,32]{0,2,1:T(8,128)S(1)}, s32[64,1,32]{0,2,1:T(8,128)}, u32[]{:S(2)}) copy-start(s32[64,1,32]{0,2,1:T(8,128)} %param.15) | copy-start | bytes 24580
  147.3 15.2 %collective-permute-start = (bf16[128,4096]{1,0:T(8,128)(2,1)S(1)}, bf16[128,4096]{1,0:T(8,128)(2,1)S(1)}, u32[]{:S(2)}, u32[]{:S(2)}) collective-permute-start(bf16[128,4096]{1,0:T(8,128)(2,1)S(1)} %shard_map.116.rows_ref), channel_id=1, source_target_pairs={{0,1},{1,0},{2,3},{3,2},{4,5},{5,4},{6,7},{7,6},{8,9},{9,8},{10,11... | collective-permute-start | bytes 3145736 | tf_op jit(solution)/shard_map/ppermute | solution.py:263

commit v5 on v4

--- a/solution.py
+++ b/solution.py
@@ -10,6 +10,7 @@
 F32 = jnp.float32
 BF16 = jnp.bfloat16
 VM = pl.BlockSpec(memory_space=pltpu.VMEM)
+ANY = pl.BlockSpec(memory_space=pl.ANY)
 SM = pl.BlockSpec(memory_space=pltpu.SMEM)
 EXTRA = 16
 
@@ -39,12 +40,12 @@
     return hi, mid, lo
 
 
-def spread(in_ref, out_ref):
+def spread(in_ref, after_ref, out_ref):
     for y in range(4):
         out_ref[y] = in_ref[...]
 
 
-def forward(count_ref, g_ref, enc_ref, dec_ref, bias_ref, dead_ref, out_ref, t_ref, stat_ref):
+def forward(count_ref, g_ref, enc_ref, bias_ref, dead_ref, out_ref, t_ref, stat_ref):
     latents = enc_ref.shape[1]
     feat = lax.axis_index("z") * 4 + lax.axis_index("y")
     row = lax.broadcasted_iota(jnp.int32, (latents, latents), 0)
@@ -71,9 +72,7 @@
     pre = jnp.dot(t_ref[...], enc_ref[...], preferred_element_type=F32) + bias_ref[...]
     feat = (jnp.maximum(pre, 0.0) * alive).astype(BF16)
     for y in range(4):
-        out_ref[y] = jnp.dot(
-            feat, dec_ref[:, pl.ds(y * 1024, 1024)], preferred_element_type=F32
-        ).astype(BF16)
+        out_ref[y] = feat
     total = jnp.zeros((8, latents), F32)
     for part in range(16):
         wide = enc_ref[pl.ds(part * 256, 256), :].astype(F32)
@@ -82,12 +81,33 @@
     stat_ref[...] = jnp.sum(norms * alive, axis=1, keepdims=True)
 
 
-def fold(in_ref, out_ref):
-    for block in range(8):
-        cols = pl.ds(block * 128, 128)
-        total = in_ref[0, :, cols].astype(F32)
+def columns(in_ref, out_ref, held_ref, in_sems, out_sems):
+    reads = [
+        pltpu.make_async_copy(
+            in_ref.at[:, pl.ds(y * 1024, 1024)], held_ref.at[y], in_sems.at[y]
+        )
+        for y in range(4)
+    ]
+    writes = [
+        pltpu.make_async_copy(held_ref.at[y], out_ref.at[y], out_sems.at[y]) for y in range(4)
+    ]
+    for y in range(4):
+        reads[y].start()
+    for y in range(4):
+        reads[y].wait()
+        writes[y].start()
+    for y in range(4):
+        writes[y].wait()
+
+
+def rebuild(feat_ref, dec_ref, out_ref):
+    for block in range(4):
+        cols = pl.ds(block * 256, 256)
+        total = jnp.dot(feat_ref[0], dec_ref[0, :, cols], preferred_element_type=F32)
         for y in range(1, 4):
-            total = total + in_ref[y, :, cols].astype(F32)
+            total = total + jnp.dot(
+                feat_ref[y], dec_ref[y, :, cols], preferred_element_type=F32
+            )
         out_ref[cols, :] = total.astype(BF16).T
 
 
@@ -226,20 +246,37 @@
 
     counts = tile_count.T
     centered = (acts.astype(F32) - dec_bias[:, None]).astype(BF16)
+    decoder = kernel_call(
+        columns,
+        shape(4, latents, width // 4),
+        [ANY],
+        0,
+        56,
+        [
+            pltpu.VMEM((4, latents, width // 4), BF16),
+            pltpu.SemaphoreType.DMA((4,)),
+            pltpu.SemaphoreType.DMA((4,)),
+        ],
+        ANY,
+    )(dec_weight)
+    decoder = exchange(decoder, "y")
     by_z = lax.all_gather(centered, "z", axis=0, tiled=True)
-    by_z = kernel_call(spread, shape(4, 16 * depth, tokens), [VM], 1 << 20, 3)(by_z)
+    by_z = kernel_call(spread, shape(4, 16 * depth, tokens), [VM, ANY], 1 << 20, 3)(
+        by_z, decoder
+    )
     gathered = exchange(by_z, "y").reshape(width, tokens)
 
-    recon, by_token, stat = kernel_call(
+    features, by_token, stat = kernel_call(
         forward,
-        (shape(4, tokens, width // 4), shape(tokens, width), shape(1, 1, dtype=F32)),
-        [SM] + [VM] * 5,
-        4 * width * latents * tokens,
-        10,
-    )(counts, gathered, enc_weight, dec_weight, enc_bias.reshape(1, latents), dead_ids)
-
-    part = exchange(recon, "y")
-    part = kernel_call(fold, shape(width // 4, tokens), [VM], 1 << 20, 3)(part)
+        (shape(4, tokens, latents), shape(tokens, width), shape(1, 1, dtype=F32)),
+        [SM] + [VM] * 4,
+        2 * width * latents * tokens,
+        8,
+    )(counts, gathered, enc_weight, enc_bias.reshape(1, latents), dead_ids)
+    features = exchange(features, "y")
+    part = kernel_call(
+        rebuild, shape(width // 4, tokens), [VM, VM], 2 * width * latents * tokens, 4
+    )(features, decoder)
     part = exchange(part.reshape(16, depth, tokens), "z")
 
     picks = kernel_call(

time: 164 us -> 161 us (0.982)
  blocking collectives: 140 us -> 130 us
  starting transfers between devices: 12.9 us -> 17.9 us
  Pallas kernels: 9.07 us -> 11 us
    all_to_all x5, blocking collectives: 108 us -> 97.7 us  [exchange(): return lax.all_to_all(value, axes, 0, 0, tiled=True)]
    all_to_all x0 -> x1, starting transfers between devices: none -> 5.02 us  [exchange(): return lax.all_to_all(value, axes, 0, 0, tiled=True)]
    pallas_call x3 -> x4, Pallas kernels: 3.63 us -> 5.57 us  [the longest x1 2.44 us: on_device(): kernel_call(columns, shape(4, latents, width // 4), [ANY], 0, 56, [pltpu....]
  transfers between devices with their start and end apart: 1 -> 2, of which waited for: 1 -> 1; matrix products, arithmetic and copies ran while one was open for 0% -> 0% of each run, Pallas kernels for 1% -> 1%
where the time goes in v5:
time: 161 us
  blocking collectives  130 us (81%)
  starting transfers between devices  17.9 us (11%)
  Pallas kernels  11 us (7%)
    all_to_all x5, blocking collectives, exchange(): return lax.all_to_all(value, axes, 0, 0, tiled=True)  97.7 us
    all_gather x1, blocking collectives, on_device(): by_z = lax.all_gather(centered, 'z', axis=0, tiled=True)  32.6 us
    ppermute x1, starting transfers between devices, on_device(): other = lax.ppermute(rows, 'core', [(0, 1), (1, 0)])  12.9 us
    all_to_all x1, starting transfers between devices, exchange(): return lax.all_to_all(value, axes, 0, 0, tiled=True)  5.02 us
  transfers between devices with their start and end apart: 2, of which 1 were waited for; matrix products, arithmetic and copies ran while one was open for 0% of the time, Pallas kernels for 1%

profile of v5, /device:TPU:1, one launch (start us, length us, event | category | flops | bytes accessed | tf_op | source)
XLA Modules:
  0.0 160.7 jit_solution(8533535191991997529)
XLA Ops:
  0.6 2.4 %shard_map.111 = bf16[4,256,1024]{2,1,0:T(8,128)(2,1)} custom-call(bf16[256,4096]{1,0:T(8,128)(2,1)} %in_ref.1), custom_call_target="tpu_custom_call" | custom-call | bytes 58720256 | tf_op jit(solution)/shard_map/pallas_call | solution.py:249
  3.1 0.0 copy-start.5
  3.1 0.0 copy-start.6
  3.1 5.0 %all-to-all-start = ((bf16[4,256,1024]{2,1,0:T(8,128)(2,1)}), bf16[4,256,1024]{2,1,0:T(8,128)(2,1)S(1)}, u32[]{:S(2)}, u32[]{:S(2)}) async-start(bf16[4,256,1024]{2,1,0:T(8,128)(2,1)} %shard_map.111), calls=%async_computation | async-start | bytes 4194304 | tf_op jit(solution)/shard_map/all_to_all | solution.py:234
  8.1 0.0 copy-done.5
  8.1 0.0 copy-done.6
  8.1 0.1 subtract_convert_fusion
  8.2 32.6 %all_gather.3.in_ref = bf16[1024,256]{1,0:T(8,128)(2,1)S(1)} all-gather(bf16[64,256]{1,0:T(8,128)(2,1)S(1)} %subtract_convert_fusion), channel_id=1, replica_groups=mesh['z'=16,'y'=4,'x'=4,'core'=2] {'z'}, dimensions={0}, use_global_device_ids=true | all-gather | bytes 557056 | tf_op jit(solution)/shard_map/all_gather | solution.py:263
  40.8 0.0 all-to-all-done.after_ref.dec_ref
  40.8 0.1 shard_map.112
  40.9 0.0 copy-start
  40.9 0.0 copy-start.1
  40.9 0.0 copy-start.3
  41.0 0.0 copy-start.4
  41.0 23.3 %all_to_all.30 = bf16[4,1024,256]{2,1,0:T(8,128)(2,1)S(1)} all-to-all(bf16[4,1024,256]{2,1,0:T(8,128)(2,1)S(1)} %shard_map.112), channel_id=1, replica_groups=mesh['z'=16,'y'=4,'x'=4,'core'=2] {'y'}, dimensions={0} | all-to-all | bytes 4194304 | tf_op jit(solution)/shard_map/all_to_all | solution.py:234
  64.2 0.0 copy-done
  64.2 0.0 copy-done.1
  64.2 0.0 copy-done.3
  64.2 0.0 copy-done.4
  64.2 2.2 %shard_map.113 = (bf16[4,256,256]{2,1,0:T(8,128)(2,1)S(1)}, bf16[256,4096]{1,0:T(8,128)(2,1)S(1)}, f32[1,1]{1,0:T(1,128)}) custom-call(s32[8,64]{1,0:T(8,128)S(1)} %bitcast.12, bf16[4096,256]{1,0:T(8,128)(2,1)S(1)} %bitcast.9, bf16[4096,256]{1,0:T(8,128)(2,1)S(1)} %copy-done, f32[1,256]{1,0:T(1,128)S(1)} %bitcast.18, s32[1,256]{1,0:T(1,128)S(1)} %copy-done.4), custom_call_target="tpu_custom_call" | custom-call | flops 536870912 | bytes 8388608 | tf_op jit(solution)/shard_map/pallas_call | solution.py:269
  66.5 9.3 %all_to_all.31.feat_ref = bf16[4,256,256]{2,1,0:T(8,128)(2,1)S(1)} all-to-all(bf16[4,256,256]{2,1,0:T(8,128)(2,1)S(1)} %get-tuple-element.11), channel_id=1, replica_groups=mesh['z'=16,'y'=4,'x'=4,'core'=2] {'y'}, dimensions={0} | all-to-all | bytes 1048576 | tf_op jit(solution)/shard_map/all_to_all | solution.py:234
  75.8 0.0 copy-start.2
  75.8 0.8 shard_map.114
  76.6 23.5 %all_to_all.32.part_ref = bf16[16,64,256]{2,1,0:T(8,128)(2,1)S(1)} all-to-all(bf16[16,64,256]{2,1,0:T(8,128)(2,1)S(1)} %bitcast.11), channel_id=1, replica_groups=mesh['z'=16,'y'=4,'x'=4,'core'=2] {'z'}, dimensions={0} | all-to-all | bytes 1048576 | tf_op jit(solution)/shard_map/all_to_all | solution.py:234
  100.1 0.0 copy-done.2
  100.1 1.1 shard_map.115
  101.2 24.5 %all_to_all.33.in_ref = bf16[16,80,128]{2,1,0:T(8,128)(2,1)S(1)} all-to-all(bf16[16,80,128]{2,1,0:T(8,128)(2,1)S(1)} %shard_map.115), channel_id=1, replica_groups=mesh['z'=16,'y'=4,'x'=4,'core'=2] {'z'}, dimensions={0} | all-to-all | bytes 655360 | tf_op jit(solution)/shard_map/all_to_all | solution.py:234
  125.7 0.2 shard_map.116
  125.9 17.1 %all_to_all.34.in_ref = bf16[16,32,1152]{2,1,0:T(8,128)(2,1)S(1)} all-to-all(bf16[16,32,1152]{2,1,0:T(8,128)(2,1)S(1)} %shard_map.116), channel_id=1, replica_groups=mesh['z'=16,'y'=4,'x'=4,'core'=2] {'y','x'}, dimensions={0} | all-to-all | bytes 2359296 | tf_op jit(solution)/shard_map/all_to_all | solution.py:234
  143.0 1.1 shard_map.117.rows_ref
  144.0 12.9 %collective-permute-start = (bf16[128,4096]{1,0:T(8,128)(2,1)S(1)}, bf16[128,4096]{1,0:T(8,128)(2,1)S(1)}, u32[]{:S(2)}, u32[]{:S(2)}) collective-permute-start(bf16[128,4096]{1,0:T(8,128)(2,1)S(1)} %shard_map.117.rows_ref), channel_id=1, source_target_pairs={{0,1},{1,0},{2,3},{3,2},{4,5},{5,4},{6,7},{7,6},{8,9},{9,8},{10,11... | collective-permute-start | bytes 3145736 | tf_op jit(solution)/shard_map/ppermute | solution.py:300
  156.9 1.6 %shard_map.118 = (bf16[32,4096]{1,0:T(8,128)(2,1)}, bf16[32,4096]{1,0:T(8,128)(2,1)}, f32[1,256]{1,0:T(1,128)}, f32[256,128]{1,0:T(8,128)S(1)}) custom-call(s32[8,64]{1,0:T(8,128)S(1)} %bitcast.15, s32[8,64]{1,0:T(8,128)S(1)} %bitcast.16, bf16[16,32,1152]{2,1,0:T(8,128)(2,1)S(1)} %all_to_all.34.in_ref, bf16[128,4096]{1,0:T(8,128)(2,1)S(1)} %shard_map.117.rows_ref, ...), custom_call_target="tpu_custom_call" | custom-call | flops 268435456 | bytes 6291456 | tf_op jit(solution)/shard_map/pallas_call | solution.py:301
  158.6 0.6 collective-permute-done.rows_ref
  159.2 1.5 shard_map.119
Async XLA Ops:
  3.1 5.1 %copy-start.5 = (bf16[64,256]{1,0:T(8,128)(2,1)S(1)}, bf16[64,256]{1,0:T(8,128)(2,1)}, u32[]{:S(2)}) copy-start(bf16[64,256]{1,0:T(8,128)(2,1)} %param.8) | copy-start | bytes 98308
  3.1 5.0 %copy-start.6 = (f32[64]{0:T(128)S(1)}, f32[64]{0:T(128)}, u32[]{:S(2)}) copy-start(f32[64]{0:T(128)} %param.9) | copy-start | bytes 772
  3.1 37.7 %all-to-all-start = ((bf16[4,256,1024]{2,1,0:T(8,128)(2,1)}), bf16[4,256,1024]{2,1,0:T(8,128)(2,1)S(1)}, u32[]{:S(2)}, u32[]{:S(2)}) async-start(bf16[4,256,1024]{2,1,0:T(8,128)(2,1)} %shard_map.111), calls=%async_computation | async-start | bytes 4194304 | tf_op jit(solution)/shard_map/all_to_all | solution.py:234
  40.9 23.3 %copy-start = (bf16[4096,256]{1,0:T(8,128)(2,1)S(1)}, bf16[4096,256]{1,0:T(8,128)(2,1)}, u32[]{:S(2)}) copy-start(bf16[4096,256]{1,0:T(8,128)(2,1)} %enc_ref.1) | copy-start | bytes 6291460
  40.9 23.3 %copy-start.1 = (s32[64,8]{0,1:T(8,128)S(1)}, s32[64,8]{0,1:T(8,128)}, u32[]{:S(2)}) copy-start(s32[64,8]{0,1:T(8,128)} %param.14) | copy-start | bytes 6148
  40.9 23.3 %copy-start.3 = (f32[256]{0:T(256)S(1)}, f32[256]{0:T(256)}, u32[]{:S(2)}) copy-start(f32[256]{0:T(256)} %param.11) | copy-start | bytes 3076
  41.0 23.3 %copy-start.4 = (s32[1,256]{1,0:T(1,128)S(1)}, s32[1,256]{1,0:T(1,128)}, u32[]{:S(2)}) copy-start(s32[1,256]{1,0:T(1,128)} %dead_ref.1) | copy-start | bytes 3076
  75.8 24.3 %copy-start.2 = (s32[64,1,32]{0,2,1:T(8,128)S(1)}, s32[64,1,32]{0,2,1:T(8,128)}, u32[]{:S(2)}) copy-start(s32[64,1,32]{0,2,1:T(8,128)} %param.15) | copy-start | bytes 24580
  144.0 15.2 %collective-permute-start = (bf16[128,4096]{1,0:T(8,128)(2,1)S(1)}, bf16[128,4096]{1,0:T(8,128)(2,1)S(1)}, u32[]{:S(2)}, u32[]{:S(2)}) collective-permute-start(bf16[128,4096]{1,0:T(8,128)(2,1)S(1)} %shard_map.117.rows_ref), channel_id=1, source_target_pairs={{0,1},{1,0},{2,3},{3,2},{4,5},{5,4},{6,7},{7,6},{8,9},{9,8},{10,11... | collective-permute-start | bytes 3145736 | tf_op jit(solution)/shard_map/ppermute | solution.py:300

commit v6 on v5

--- a/solution.py
+++ b/solution.py
@@ -11,7 +11,6 @@
 BF16 = jnp.bfloat16
 VM = pl.BlockSpec(memory_space=pltpu.VMEM)
 ANY = pl.BlockSpec(memory_space=pl.ANY)
-SM = pl.BlockSpec(memory_space=pltpu.SMEM)
 EXTRA = 16
 
 
@@ -45,15 +44,22 @@
         out_ref[y] = in_ref[...]
 
 
-def forward(count_ref, g_ref, enc_ref, bias_ref, dead_ref, out_ref, t_ref, stat_ref):
+def own_counts(counts_ref):
+    counts = counts_ref[...]
+    feat = lax.axis_index("z") * 4 + lax.axis_index("y")
+    shard = lax.broadcasted_iota(jnp.int32, counts.shape, 1)
+    return jnp.sum(jnp.where(shard == feat, counts, 0), axis=1, keepdims=True)
+
+
+def forward(counts_ref, g_ref, enc_ref, bias_ref, dead_ref, out_ref, t_ref, stat_ref):
     latents = enc_ref.shape[1]
-    feat = lax.axis_index("z") * 4 + lax.axis_index("y")
+    count = own_counts(counts_ref)
     row = lax.broadcasted_iota(jnp.int32, (latents, latents), 0)
     col = lax.broadcasted_iota(jnp.int32, (latents, latents), 1)
     slot = lax.broadcasted_iota(jnp.int32, (latents, 1), 0)
     limit = jnp.zeros((latents, 1), jnp.int32)
     for t in range(8):
-        limit = jnp.where(slot // 32 == t, count_ref[t, feat], limit)
+        limit = jnp.where(slot // 32 == t, count[t : t + 1], limit)
     dead = jnp.sum(jnp.where(row == col, dead_ref[...], 0), axis=1, keepdims=True)
     dead = jnp.where(slot % 32 < limit, dead, -1)
     alive = 1.0 - jnp.max(jnp.where(dead == col, 1.0, 0.0), axis=0, keepdims=True)
@@ -78,7 +84,8 @@
         wide = enc_ref[pl.ds(part * 256, 256), :].astype(F32)
         total = total + jnp.sum((wide * wide).reshape(32, 8, latents), axis=0)
     norms = jnp.sqrt(jnp.sum(total, axis=0, keepdims=True))
-    stat_ref[...] = jnp.sum(norms * alive, axis=1, keepdims=True)
+    stat = jnp.sum(norms * alive, axis=1, keepdims=True)
+    stat_ref[...] = jnp.broadcast_to(stat, stat_ref.shape)
 
 
 def columns(in_ref, out_ref, held_ref, in_sems, out_sems):
@@ -120,7 +127,7 @@
     error = own.astype(F32) - recon
     loss = jnp.sum(error * error, axis=0, keepdims=True)
     loss = jnp.concatenate([loss[:, :128], loss[:, 128:]], 0)
-    stat = jnp.broadcast_to(stat_ref[...], (2, 128))
+    stat = stat_ref[pl.ds(0, 2), :]
     pad = jnp.zeros((4, 128), F32)
     pieces = [split3(v) for v in (loss, stat)]
     extra = jnp.concatenate([p.astype(F32) for s in pieces for p in s] + [pad], 0).astype(BF16)
@@ -183,28 +190,33 @@
     return jnp.concatenate([loss[0:1], loss[1:2]], 1), gain
 
 
-def normalise(count_ref, counts_ref, in_ref, rows_ref):
-    feat = lax.axis_index("z") * 4 + lax.axis_index("y")
+def tile_count(count, t):
+    tile = lax.broadcasted_iota(jnp.int32, count.shape, 0)
+    return jnp.sum(jnp.where(tile == t, count, 0), axis=0, keepdims=True)
+
+
+def normalise(counts_ref, in_ref, rows_ref):
     core = lax.axis_index("core")
+    count = own_counts(counts_ref)
     _, gain = read_riders(counts_ref, in_ref, 0)
     for x in range(4):
-        scale = tile_scale(in_ref, count_ref[x * 2 + core, feat], x)
+        scale = tile_scale(in_ref, tile_count(count, x * 2 + core), x)
         for y in range(4):
             unit = in_ref[y * 4 + x, :, pl.ds(0, 1024)].astype(F32) * scale
             rows_ref[pl.ds(x * 32, 32), pl.ds(y * 1024, 1024)] = (gain * unit).astype(BF16)
 
 
-def finish(count_ref, counts_ref, in_ref, rows_ref, t_ref, enc_ref, dec_ref, loss_ref, half_ref):
-    feat = lax.axis_index("z") * 4 + lax.axis_index("y")
+def finish(counts_ref, in_ref, rows_ref, t_ref, enc_ref, dec_ref, loss_ref, half_ref):
     x_own = lax.axis_index("x")
     core = lax.axis_index("core")
+    count = own_counts(counts_ref)
     loss, _ = read_riders(counts_ref, in_ref, x_own)
     loss_ref[...] = loss * (1.0 / 4096.0)
     for x in range(4):
 
         @pl.when(x == x_own)
         def _(x=x):
-            scale = tile_scale(in_ref, count_ref[x * 2 + core, feat], x)
+            scale = tile_scale(in_ref, tile_count(count, x * 2 + core), x)
             for y in range(4):
                 cols = pl.ds(y * 1024, 1024)
                 unit = in_ref[y * 4 + x, :, pl.ds(0, 1024)].astype(F32) * scale
@@ -268,8 +280,8 @@
 
     features, by_token, stat = kernel_call(
         forward,
-        (shape(4, tokens, latents), shape(tokens, width), shape(1, 1, dtype=F32)),
-        [SM] + [VM] * 4,
+        (shape(4, tokens, latents), shape(tokens, width), shape(8, 128, dtype=F32)),
+        [VM] * 5,
         2 * width * latents * tokens,
         8,
     )(counts, gathered, enc_weight, enc_bias.reshape(1, latents), dead_ids)
@@ -294,9 +306,7 @@
     picks = exchange(picks, "z")
     picks = kernel_call(relay, shape(16, tile, width // 4 + 128), [VM], 1 << 20, 2)(picks)
     picks = exchange(picks, ("y", "x"))
-    rows = kernel_call(normalise, shape(4 * tile, width), [SM, VM, VM], 1 << 21, 3)(
-        counts, counts, picks
-    )
+    rows = kernel_call(normalise, shape(4 * tile, width), [VM, VM], 1 << 21, 3)(counts, picks)
     other = lax.ppermute(rows, "core", [(0, 1), (1, 0)])
     new_enc, new_dec, token_loss, half = kernel_call(
         finish,
@@ -306,10 +316,10 @@
             shape(1, tokens, dtype=F32),
             shape(tokens, 4 * tile, dtype=F32),
         ),
-        [SM] + [VM] * 4,
+        [VM] * 4,
         tokens * slots * width,
         6,
-    )(counts, counts, picks, rows, by_token)
+    )(counts, picks, rows, by_token)
     reencoded = kernel_call(
         reencode, shape(tokens, slots), [VM] * 3, tokens * slots * width, 4
     )(other, by_token, half)

time: 161 us -> 159 us (0.988)
  Pallas kernels: 11 us -> 8.13 us
where the time goes in v6:
time: 159 us; the launch traced here: 158 us
  blocking collectives  130 us (82%)
  starting transfers between devices  17.9 us (11%)
  Pallas kernels  8.13 us (5%)
    all_to_all x5, blocking collectives, exchange(): return lax.all_to_all(value, axes, 0, 0, tiled=True)  97.7 us
    all_gather x1, blocking collectives, on_device(): by_z = lax.all_gather(centered, 'z', axis=0, tiled=True)  32.6 us
    ppermute x1, starting transfers between devices, on_device(): other = lax.ppermute(rows, 'core', [(0, 1), (1, 0)])  12.9 us
    all_to_all x1, starting transfers between devices, exchange(): return lax.all_to_all(value, axes, 0, 0, tiled=True)  5.02 us
  transfers between devices with their start and end apart: 2, of which 1 were waited for; matrix products, arithmetic and copies ran while one was open for 0% of the time, Pallas kernels for 1%

profile of v6, /device:TPU:1, one launch (start us, length us, event | category | flops | bytes accessed | tf_op | source)
XLA Modules:
  0.0 158.3 jit_solution(12687384131585134965)
XLA Ops:
  0.6 2.4 %shard_map.111 = bf16[4,256,1024]{2,1,0:T(8,128)(2,1)} custom-call(bf16[256,4096]{1,0:T(8,128)(2,1)} %in_ref.1), custom_call_target="tpu_custom_call" | custom-call | bytes 58720256 | tf_op jit(solution)/shard_map/pallas_call | solution.py:261
  3.1 0.0 copy-start.5
  3.1 0.0 copy-start.6
  3.1 5.0 %all-to-all-start = ((bf16[4,256,1024]{2,1,0:T(8,128)(2,1)}), bf16[4,256,1024]{2,1,0:T(8,128)(2,1)S(1)}, u32[]{:S(2)}, u32[]{:S(2)}) async-start(bf16[4,256,1024]{2,1,0:T(8,128)(2,1)} %shard_map.111), calls=%async_computation | async-start | bytes 4194304 | tf_op jit(solution)/shard_map/all_to_all | solution.py:246
  8.1 0.0 copy-done.5
  8.1 0.0 copy-done.6
  8.1 0.1 subtract_convert_fusion
  8.2 32.6 %all_gather.3.in_ref = bf16[1024,256]{1,0:T(8,128)(2,1)S(1)} all-gather(bf16[64,256]{1,0:T(8,128)(2,1)S(1)} %subtract_convert_fusion), channel_id=1, replica_groups=mesh['z'=16,'y'=4,'x'=4,'core'=2] {'z'}, dimensions={0}, use_global_device_ids=true | all-gather | bytes 557056 | tf_op jit(solution)/shard_map/all_gather | solution.py:275
  40.8 0.0 all-to-all-done.after_ref.dec_ref
  40.8 0.1 shard_map.112
  40.9 0.0 copy-start
  40.9 0.0 copy-start.1
  40.9 0.0 copy-start.3
  41.0 0.0 copy-start.4
  41.0 23.3 %all_to_all.30 = bf16[4,1024,256]{2,1,0:T(8,128)(2,1)S(1)} all-to-all(bf16[4,1024,256]{2,1,0:T(8,128)(2,1)S(1)} %shard_map.112), channel_id=1, replica_groups=mesh['z'=16,'y'=4,'x'=4,'core'=2] {'y'}, dimensions={0} | all-to-all | bytes 4194304 | tf_op jit(solution)/shard_map/all_to_all | solution.py:246
  64.2 0.0 copy-done
  64.2 0.0 copy-done.1
  64.2 0.0 copy-done.3
  64.2 0.0 copy-done.4
  64.2 1.1 shard_map.113
  65.3 9.3 %all_to_all.31.feat_ref = bf16[4,256,256]{2,1,0:T(8,128)(2,1)S(1)} all-to-all(bf16[4,256,256]{2,1,0:T(8,128)(2,1)S(1)} %get-tuple-element.11), channel_id=1, replica_groups=mesh['z'=16,'y'=4,'x'=4,'core'=2] {'y'}, dimensions={0} | all-to-all | bytes 1048576 | tf_op jit(solution)/shard_map/all_to_all | solution.py:246
  74.7 0.0 copy-start.2
  74.7 0.8 shard_map.114
  75.5 23.5 %all_to_all.32.part_ref = bf16[16,64,256]{2,1,0:T(8,128)(2,1)S(1)} all-to-all(bf16[16,64,256]{2,1,0:T(8,128)(2,1)S(1)} %bitcast.11), channel_id=1, replica_groups=mesh['z'=16,'y'=4,'x'=4,'core'=2] {'z'}, dimensions={0} | all-to-all | bytes 1048576 | tf_op jit(solution)/shard_map/all_to_all | solution.py:246
  99.0 0.0 copy-done.2
  99.0 0.4 shard_map.115
  99.4 24.5 %all_to_all.33.in_ref = bf16[16,80,128]{2,1,0:T(8,128)(2,1)S(1)} all-to-all(bf16[16,80,128]{2,1,0:T(8,128)(2,1)S(1)} %shard_map.115), channel_id=1, replica_groups=mesh['z'=16,'y'=4,'x'=4,'core'=2] {'z'}, dimensions={0} | all-to-all | bytes 655360 | tf_op jit(solution)/shard_map/all_to_all | solution.py:246
  123.9 0.2 shard_map.116
  124.1 17.1 %all_to_all.34.in_ref = bf16[16,32,1152]{2,1,0:T(8,128)(2,1)S(1)} all-to-all(bf16[16,32,1152]{2,1,0:T(8,128)(2,1)S(1)} %shard_map.116), channel_id=1, replica_groups=mesh['z'=16,'y'=4,'x'=4,'core'=2] {'y','x'}, dimensions={0} | all-to-all | bytes 2359296 | tf_op jit(solution)/shard_map/all_to_all | solution.py:246
  141.1 0.5 shard_map.117.rows_ref
  141.7 12.9 %collective-permute-start = (bf16[128,4096]{1,0:T(8,128)(2,1)S(1)}, bf16[128,4096]{1,0:T(8,128)(2,1)S(1)}, u32[]{:S(2)}, u32[]{:S(2)}) collective-permute-start(bf16[128,4096]{1,0:T(8,128)(2,1)S(1)} %shard_map.117.rows_ref), channel_id=1, source_target_pairs={{0,1},{1,0},{2,3},{3,2},{4,5},{5,4},{6,7},{7,6},{8,9},{9,8},{10,11... | collective-permute-start | bytes 3145736 | tf_op jit(solution)/shard_map/ppermute | solution.py:310
  154.6 1.1 shard_map.118
  155.7 1.2 collective-permute-done.rows_ref
  156.9 1.5 shard_map.119
Async XLA Ops:
  3.1 5.1 %copy-start.5 = (bf16[64,256]{1,0:T(8,128)(2,1)S(1)}, bf16[64,256]{1,0:T(8,128)(2,1)}, u32[]{:S(2)}) copy-start(bf16[64,256]{1,0:T(8,128)(2,1)} %param.8) | copy-start | bytes 98308
  3.1 5.0 %copy-start.6 = (f32[64]{0:T(128)S(1)}, f32[64]{0:T(128)}, u32[]{:S(2)}) copy-start(f32[64]{0:T(128)} %param.9) | copy-start | bytes 772
  3.1 37.7 %all-to-all-start = ((bf16[4,256,1024]{2,1,0:T(8,128)(2,1)}), bf16[4,256,1024]{2,1,0:T(8,128)(2,1)S(1)}, u32[]{:S(2)}, u32[]{:S(2)}) async-start(bf16[4,256,1024]{2,1,0:T(8,128)(2,1)} %shard_map.111), calls=%async_computation | async-start | bytes 4194304 | tf_op jit(solution)/shard_map/all_to_all | solution.py:246
  40.9 23.3 %copy-start = (bf16[4096,256]{1,0:T(8,128)(2,1)S(1)}, bf16[4096,256]{1,0:T(8,128)(2,1)}, u32[]{:S(2)}) copy-start(bf16[4096,256]{1,0:T(8,128)(2,1)} %enc_ref.1) | copy-start | bytes 6291460
  40.9 23.3 %copy-start.1 = (s32[64,8]{0,1:T(8,128)S(1)}, s32[64,8]{0,1:T(8,128)}, u32[]{:S(2)}) copy-start(s32[64,8]{0,1:T(8,128)} %param.14) | copy-start | bytes 6148
  40.9 23.3 %copy-start.3 = (f32[256]{0:T(256)S(1)}, f32[256]{0:T(256)}, u32[]{:S(2)}) copy-start(f32[256]{0:T(256)} %param.11) | copy-start | bytes 3076
  41.0 23.3 %copy-start.4 = (s32[1,256]{1,0:T(1,128)S(1)}, s32[1,256]{1,0:T(1,128)}, u32[]{:S(2)}) copy-start(s32[1,256]{1,0:T(1,128)} %dead_ref.1) | copy-start | bytes 3076
  74.7 24.3 %copy-start.2 = (s32[64,1,32]{0,2,1:T(8,128)S(1)}, s32[64,1,32]{0,2,1:T(8,128)}, u32[]{:S(2)}) copy-start(s32[64,1,32]{0,2,1:T(8,128)} %param.15) | copy-start | bytes 24580
  141.7 15.2 %collective-permute-start = (bf16[128,4096]{1,0:T(8,128)(2,1)S(1)}, bf16[128,4096]{1,0:T(8,128)(2,1)S(1)}, u32[]{:S(2)}, u32[]{:S(2)}) collective-permute-start(bf16[128,4096]{1,0:T(8,128)(2,1)S(1)} %shard_map.117.rows_ref), channel_id=1, source_target_pairs={{0,1},{1,0},{2,3},{3,2},{4,5},{5,4},{6,7},{7,6},{8,9},{9,8},{10,11... | collective-permute-start | bytes 3145736 | tf_op jit(solution)/shard_map/ppermute | solution.py:310

commit v7 on v6

--- a/solution.py
+++ b/solution.py
@@ -89,29 +89,34 @@
 
 
 def columns(in_ref, out_ref, held_ref, in_sems, out_sems):
-    reads = [
-        pltpu.make_async_copy(
-            in_ref.at[:, pl.ds(y * 1024, 1024)], held_ref.at[y], in_sems.at[y]
+    own = lax.axis_index("y")
+    reads, writes = [], []
+    for k in range(1, 4):
+        y = lax.rem(own + k, 4)
+        cols = pl.ds(pl.multiple_of(y * 1024, 1024), 1024)
+        reads.append(
+            pltpu.make_async_copy(in_ref.at[:, cols], held_ref.at[k - 1], in_sems.at[k - 1])
         )
-        for y in range(4)
-    ]
-    writes = [
-        pltpu.make_async_copy(held_ref.at[y], out_ref.at[y], out_sems.at[y]) for y in range(4)
-    ]
-    for y in range(4):
-        reads[y].start()
-    for y in range(4):
-        reads[y].wait()
-        writes[y].start()
-    for y in range(4):
-        writes[y].wait()
-
-
-def rebuild(feat_ref, dec_ref, out_ref):
+        writes.append(
+            pltpu.make_async_copy(held_ref.at[k - 1], out_ref.at[y], out_sems.at[k - 1])
+        )
+    for read in reads:
+        read.start()
+    for read, write in zip(reads, writes):
+        read.wait()
+        write.start()
+    for write in writes:
+        write.wait()
+
+
+def rebuild(feat_ref, dec_ref, own_ref, out_ref):
+    own = lax.axis_index("y")
     for block in range(4):
         cols = pl.ds(block * 256, 256)
-        total = jnp.dot(feat_ref[0], dec_ref[0, :, cols], preferred_element_type=F32)
-        for y in range(1, 4):
+        mine = pl.ds(pl.multiple_of(own * 1024 + block * 256, 256), 256)
+        total = jnp.dot(feat_ref[own], own_ref[:, mine], preferred_element_type=F32)
+        for k in range(1, 4):
+            y = lax.rem(own + k, 4)
             total = total + jnp.dot(
                 feat_ref[y], dec_ref[y, :, cols], preferred_element_type=F32
             )
@@ -265,9 +270,9 @@
         0,
         56,
         [
-            pltpu.VMEM((4, latents, width // 4), BF16),
-            pltpu.SemaphoreType.DMA((4,)),
-            pltpu.SemaphoreType.DMA((4,)),
+            pltpu.VMEM((3, latents, width // 4), BF16),
+            pltpu.SemaphoreType.DMA((3,)),
+            pltpu.SemaphoreType.DMA((3,)),
         ],
         ANY,
     )(dec_weight)
@@ -287,8 +292,8 @@
     )(counts, gathered, enc_weight, enc_bias.reshape(1, latents), dead_ids)
     features = exchange(features, "y")
     part = kernel_call(
-        rebuild, shape(width // 4, tokens), [VM, VM], 2 * width * latents * tokens, 4
-    )(features, decoder)
+        rebuild, shape(width // 4, tokens), [VM] * 3, 2 * width * latents * tokens, 6
+    )(features, decoder, dec_weight)
     part = exchange(part.reshape(16, depth, tokens), "z")
 
     picks = kernel_call(

time: 159 us -> 159 us (level)
  no operation moved by 1% of the time
where the time goes in v7:
time: 159 us; the launch traced here: 158 us
  blocking collectives  130 us (82%)
  starting transfers between devices  17.9 us (11%)
  Pallas kernels  7.98 us (5%)
    all_to_all x5, blocking collectives, exchange(): return lax.all_to_all(value, axes, 0, 0, tiled=True)  97.7 us
    all_gather x1, blocking collectives, on_device(): by_z = lax.all_gather(centered, 'z', axis=0, tiled=True)  32.6 us
    ppermute x1, starting transfers between devices, on_device(): other = lax.ppermute(rows, 'core', [(0, 1), (1, 0)])  12.9 us
    all_to_all x1, starting transfers between devices, exchange(): return lax.all_to_all(value, axes, 0, 0, tiled=True)  4.99 us
  transfers between devices with their start and end apart: 2, of which 1 were waited for; matrix products, arithmetic and copies ran while one was open for 0% of the time, Pallas kernels for 1%

profile of v7, /device:TPU:1, one launch (start us, length us, event | category | flops | bytes accessed | tf_op | source)
XLA Modules:
  0.0 158.2 jit_solution(6196464660443051266)
XLA Ops:
  0.6 2.3 %shard_map.111 = bf16[4,256,1024]{2,1,0:T(8,128)(2,1)} custom-call(bf16[256,4096]{1,0:T(8,128)(2,1)} %own_ref.1), custom_call_target="tpu_custom_call" | custom-call | bytes 58720256 | tf_op jit(solution)/shard_map/pallas_call | solution.py:266
  2.9 0.0 copy-start.6
  2.9 0.0 copy-start.7
  2.9 5.0 %all-to-all-start = ((bf16[4,256,1024]{2,1,0:T(8,128)(2,1)}), bf16[4,256,1024]{2,1,0:T(8,128)(2,1)S(1)}, u32[]{:S(2)}, u32[]{:S(2)}) async-start(bf16[4,256,1024]{2,1,0:T(8,128)(2,1)} %shard_map.111), calls=%async_computation | async-start | bytes 4194304 | tf_op jit(solution)/shard_map/all_to_all | solution.py:251
  7.9 0.0 copy-done.6
  7.9 0.0 copy-done.7
  7.9 0.1 subtract_convert_fusion
  8.0 32.6 %all_gather.3.in_ref = bf16[1024,256]{1,0:T(8,128)(2,1)S(1)} all-gather(bf16[64,256]{1,0:T(8,128)(2,1)S(1)} %subtract_convert_fusion), channel_id=1, replica_groups=mesh['z'=16,'y'=4,'x'=4,'core'=2] {'z'}, dimensions={0}, use_global_device_ids=true | all-gather | bytes 557056 | tf_op jit(solution)/shard_map/all_gather | solution.py:280
  40.6 0.0 all-to-all-done.after_ref.dec_ref
  40.6 0.1 shard_map.112
  40.7 0.0 copy-start.1
  40.7 0.0 copy-start.2
  40.7 0.0 copy-start.4
  40.8 0.0 copy-start.5
  40.8 23.3 %all_to_all.30 = bf16[4,1024,256]{2,1,0:T(8,128)(2,1)S(1)} all-to-all(bf16[4,1024,256]{2,1,0:T(8,128)(2,1)S(1)} %shard_map.112), channel_id=1, replica_groups=mesh['z'=16,'y'=4,'x'=4,'core'=2] {'y'}, dimensions={0} | all-to-all | bytes 4194304 | tf_op jit(solution)/shard_map/all_to_all | solution.py:251
  64.0 0.0 copy-done.1
  64.0 0.0 copy-done.2
  64.0 0.0 copy-done.4
  64.0 0.0 copy-done.5
  64.0 0.0 copy-start
  64.1 1.1 shard_map.113
  65.2 9.3 %all_to_all.31.feat_ref = bf16[4,256,256]{2,1,0:T(8,128)(2,1)S(1)} all-to-all(bf16[4,256,256]{2,1,0:T(8,128)(2,1)S(1)} %get-tuple-element.11), channel_id=1, replica_groups=mesh['z'=16,'y'=4,'x'=4,'core'=2] {'y'}, dimensions={0} | all-to-all | bytes 1048576 | tf_op jit(solution)/shard_map/all_to_all | solution.py:251
  74.5 0.0 copy-done
  74.5 0.0 copy-start.3
  74.5 0.8 shard_map.114
  75.3 23.5 %all_to_all.32.part_ref = bf16[16,64,256]{2,1,0:T(8,128)(2,1)S(1)} all-to-all(bf16[16,64,256]{2,1,0:T(8,128)(2,1)S(1)} %bitcast.11), channel_id=1, replica_groups=mesh['z'=16,'y'=4,'x'=4,'core'=2] {'z'}, dimensions={0} | all-to-all | bytes 1048576 | tf_op jit(solution)/shard_map/all_to_all | solution.py:251
  98.8 0.0 copy-done.3
  98.8 0.4 shard_map.115
  99.2 24.5 %all_to_all.33.in_ref = bf16[16,80,128]{2,1,0:T(8,128)(2,1)S(1)} all-to-all(bf16[16,80,128]{2,1,0:T(8,128)(2,1)S(1)} %shard_map.115), channel_id=1, replica_groups=mesh['z'=16,'y'=4,'x'=4,'core'=2] {'z'}, dimensions={0} | all-to-all | bytes 655360 | tf_op jit(solution)/shard_map/all_to_all | solution.py:251
  123.7 0.2 shard_map.116
  123.9 17.1 %all_to_all.34.in_ref = bf16[16,32,1152]{2,1,0:T(8,128)(2,1)S(1)} all-to-all(bf16[16,32,1152]{2,1,0:T(8,128)(2,1)S(1)} %shard_map.116), channel_id=1, replica_groups=mesh['z'=16,'y'=4,'x'=4,'core'=2] {'y','x'}, dimensions={0} | all-to-all | bytes 2359296 | tf_op jit(solution)/shard_map/all_to_all | solution.py:251
  141.0 0.5 shard_map.117.rows_ref
  141.5 12.9 %collective-permute-start = (bf16[128,4096]{1,0:T(8,128)(2,1)S(1)}, bf16[128,4096]{1,0:T(8,128)(2,1)S(1)}, u32[]{:S(2)}, u32[]{:S(2)}) collective-permute-start(bf16[128,4096]{1,0:T(8,128)(2,1)S(1)} %shard_map.117.rows_ref), channel_id=1, source_target_pairs={{0,1},{1,0},{2,3},{3,2},{4,5},{5,4},{6,7},{7,6},{8,9},{9,8},{10,11... | collective-permute-start | bytes 3145736 | tf_op jit(solution)/shard_map/ppermute | solution.py:315
  154.4 1.1 shard_map.118
  155.5 1.2 collective-permute-done.rows_ref
  156.7 1.5 shard_map.119
Async XLA Ops:
  2.9 5.0 %copy-start.6 = (bf16[64,256]{1,0:T(8,128)(2,1)S(1)}, bf16[64,256]{1,0:T(8,128)(2,1)}, u32[]{:S(2)}) copy-start(bf16[64,256]{1,0:T(8,128)(2,1)} %param.8) | copy-start | bytes 98308
  2.9 5.0 %copy-start.7 = (f32[64]{0:T(128)S(1)}, f32[64]{0:T(128)}, u32[]{:S(2)}) copy-start(f32[64]{0:T(128)} %param.9) | copy-start | bytes 772
  2.9 37.6 %all-to-all-start = ((bf16[4,256,1024]{2,1,0:T(8,128)(2,1)}), bf16[4,256,1024]{2,1,0:T(8,128)(2,1)S(1)}, u32[]{:S(2)}, u32[]{:S(2)}) async-start(bf16[4,256,1024]{2,1,0:T(8,128)(2,1)} %shard_map.111), calls=%async_computation | async-start | bytes 4194304 | tf_op jit(solution)/shard_map/all_to_all | solution.py:251
  40.7 23.3 %copy-start.1 = (bf16[4096,256]{1,0:T(8,128)(2,1)S(1)}, bf16[4096,256]{1,0:T(8,128)(2,1)}, u32[]{:S(2)}) copy-start(bf16[4096,256]{1,0:T(8,128)(2,1)} %enc_ref.1) | copy-start | bytes 6291460
  40.7 23.3 %copy-start.2 = (s32[64,8]{0,1:T(8,128)S(1)}, s32[64,8]{0,1:T(8,128)}, u32[]{:S(2)}) copy-start(s32[64,8]{0,1:T(8,128)} %param.14) | copy-start | bytes 6148
  40.7 23.3 %copy-start.4 = (f32[256]{0:T(256)S(1)}, f32[256]{0:T(256)}, u32[]{:S(2)}) copy-start(f32[256]{0:T(256)} %param.11) | copy-start | bytes 3076
  40.8 23.3 %copy-start.5 = (s32[1,256]{1,0:T(1,128)S(1)}, s32[1,256]{1,0:T(1,128)}, u32[]{:S(2)}) copy-start(s32[1,256]{1,0:T(1,128)} %dead_ref.1) | copy-start | bytes 3076
  64.0 10.4 %copy-start = (bf16[256,4096]{1,0:T(8,128)(2,1)S(1)}, bf16[256,4096]{1,0:T(8,128)(2,1)}, u32[]{:S(2)}) copy-start(bf16[256,4096]{1,0:T(8,128)(2,1)} %own_ref.1) | copy-start | bytes 6291460
  74.5 24.3 %copy-start.3 = (s32[64,1,32]{0,2,1:T(8,128)S(1)}, s32[64,1,32]{0,2,1:T(8,128)}, u32[]{:S(2)}) copy-start(s32[64,1,32]{0,2,1:T(8,128)} %param.15) | copy-start | bytes 24580
  141.5 15.2 %collective-permute-start = (bf16[128,4096]{1,0:T(8,128)(2,1)S(1)}, bf16[128,4096]{1,0:T(8,128)(2,1)S(1)}, u32[]{:S(2)}, u32[]{:S(2)}) collective-permute-start(bf16[128,4096]{1,0:T(8,128)(2,1)S(1)} %shard_map.117.rows_ref), channel_id=1, source_target_pairs={{0,1},{1,0},{2,3},{3,2},{4,5},{5,4},{6,7},{7,6},{8,9},{9,8},{10,11... | collective-permute-start | bytes 3145736 | tf_op jit(solution)/shard_map/ppermute | solution.py:315

commit v8 on v7

--- a/solution.py
+++ b/solution.py
@@ -12,6 +12,7 @@
 VM = pl.BlockSpec(memory_space=pltpu.VMEM)
 ANY = pl.BlockSpec(memory_space=pl.ANY)
 EXTRA = 16
+Z_ORDER = [(i + 8) % 16 for i in range(16)]
 
 
 def kernel_call(body, out_shape, in_specs, flops, mib, scratch=(), out_specs=None):
@@ -120,7 +121,7 @@
             total = total + jnp.dot(
                 feat_ref[y], dec_ref[y, :, cols], preferred_element_type=F32
             )
-        out_ref[cols, :] = total.astype(BF16).T
+        out_ref[pl.ds((block + 2) % 4 * 256, 256), :] = total.astype(BF16).T
 
 
 def residual(part_ref, g_ref, sample_ref, stat_ref, out_ref):
@@ -146,8 +147,8 @@
         wanted = jnp.sum(wide[z * 4 : z * 4 + 4], axis=0, keepdims=True)
         onehot = jnp.where(token == wanted, 1.0, 0.0).astype(BF16)
         picked = jnp.dot(error_b, onehot, preferred_element_type=F32)
-        out_ref[z, pl.ds(0, 64), :] = picked.astype(BF16)
-        out_ref[z, pl.ds(64, EXTRA), :] = extra
+        out_ref[(z + 8) % 16, pl.ds(0, 64), :] = picked.astype(BF16)
+        out_ref[(z + 8) % 16, pl.ds(64, EXTRA), :] = extra
 
 
 def relay(in_ref, out_ref):
@@ -163,8 +164,9 @@
     pieces = [p.astype(F32) for v in (loss, stat) for p in split3(v)]
     riders = jnp.concatenate(pieces + [jnp.zeros((20, 128), F32)], 0).astype(BF16)
     for pair in range(8):
+        first = (2 * pair + 8) % 16
         both = jnp.concatenate(
-            [in_ref[2 * pair, pl.ds(0, 64), :], in_ref[2 * pair + 1, pl.ds(0, 64), :]], 0
+            [in_ref[first, pl.ds(0, 64), :], in_ref[first + 1, pl.ds(0, 64), :]], 0
         ).T
         for y in range(4):
             for x in range(4):
@@ -249,6 +251,10 @@
 
 def exchange(value, axes):
     return lax.all_to_all(value, axes, 0, 0, tiled=True)
+
+
+def exchange_z(value):
+    return lax.all_to_all(value, "z", 0, 0, axis_index_groups=[Z_ORDER], tiled=True)
 
 
 def shape(*dims, dtype=BF16):
@@ -294,7 +300,7 @@
     part = kernel_call(
         rebuild, shape(width // 4, tokens), [VM] * 3, 2 * width * latents * tokens, 6
     )(features, decoder, dec_weight)
-    part = exchange(part.reshape(16, depth, tokens), "z")
+    part = exchange_z(part.reshape(16, depth, tokens))
 
     picks = kernel_call(
         residual,
@@ -308,7 +314,7 @@
         sample_rows.transpose(1, 2, 0).reshape(tile, 64),
         stat,
     )
-    picks = exchange(picks, "z")
+    picks = exchange_z(picks)
     picks = kernel_call(relay, shape(16, tile, width // 4 + 128), [VM], 1 << 20, 2)(picks)
     picks = exchange(picks, ("y", "x"))
     rows = kernel_call(normalise, shape(4 * tile, width), [VM, VM], 1 << 21, 3)(counts, picks)

time: 159 us -> 159 us (level)
  blocking collectives: 130 us -> 133 us
  starting transfers between devices: 17.9 us -> 15 us
    all_to_all x0 -> x2, blocking collectives: none -> 48.1 us  [exchange_z(): lax.all_to_all(value, 'z', 0, 0, axis_index_groups=[Z_ORDER], tiled=True)]
    all_to_all x5 -> x3, blocking collectives: 97.7 us -> 52.4 us  [exchange(): return lax.all_to_all(value, axes, 0, 0, tiled=True)]
    ppermute x1, starting transfers between devices: 12.9 us -> 10 us  [on_device(): other = lax.ppermute(rows, 'core', [(0, 1), (1, 0)])]
where the time goes in v8:
time: 159 us; the launch traced here: 158 us
  blocking collectives  133 us (84%)
  starting transfers between devices  15 us (9%)
  Pallas kernels  7.98 us (5%)
    all_to_all x3, blocking collectives, exchange(): return lax.all_to_all(value, axes, 0, 0, tiled=True)  52.4 us
    all_to_all x2, blocking collectives, exchange_z(): lax.all_to_all(value, 'z', 0, 0, axis_index_groups=[Z_ORDER], tiled=True)  48.1 us
    all_gather x1, blocking collectives, on_device(): by_z = lax.all_gather(centered, 'z', axis=0, tiled=True)  32.6 us
    ppermute x1, starting transfers between devices, on_device(): other = lax.ppermute(rows, 'core', [(0, 1), (1, 0)])  10 us
    all_to_all x1, starting transfers between devices, exchange(): return lax.all_to_all(value, axes, 0, 0, tiled=True)  4.99 us
  transfers between devices with their start and end apart: 2, of which 1 were waited for; matrix products, arithmetic and copies ran while one was open for 0% of the time, Pallas kernels for 1%

profile of v8, /device:TPU:1, one launch (start us, length us, event | category | flops | bytes accessed | tf_op | source)
XLA Modules:
  0.0 158.1 jit_solution(594325794991350045)
XLA Ops:
  0.6 2.3 %shard_map.111 = bf16[4,256,1024]{2,1,0:T(8,128)(2,1)} custom-call(bf16[256,4096]{1,0:T(8,128)(2,1)} %own_ref.1), custom_call_target="tpu_custom_call" | custom-call | bytes 58720256 | tf_op jit(solution)/shard_map/pallas_call | solution.py:272
  2.9 0.0 copy-start.6
  2.9 0.0 copy-start.7
  2.9 5.0 %all-to-all-start = ((bf16[4,256,1024]{2,1,0:T(8,128)(2,1)}), bf16[4,256,1024]{2,1,0:T(8,128)(2,1)S(1)}, u32[]{:S(2)}, u32[]{:S(2)}) async-start(bf16[4,256,1024]{2,1,0:T(8,128)(2,1)} %shard_map.111), calls=%async_computation | async-start | bytes 4194304 | tf_op jit(solution)/shard_map/all_to_all | solution.py:253
  7.9 0.0 copy-done.6
  7.9 0.0 copy-done.7
  7.9 0.1 subtract_convert_fusion
  8.0 32.6 %all_gather.3.in_ref = bf16[1024,256]{1,0:T(8,128)(2,1)S(1)} all-gather(bf16[64,256]{1,0:T(8,128)(2,1)S(1)} %subtract_convert_fusion), channel_id=1, replica_groups=mesh['z'=16,'y'=4,'x'=4,'core'=2] {'z'}, dimensions={0}, use_global_device_ids=true | all-gather | bytes 557056 | tf_op jit(solution)/shard_map/all_gather | solution.py:286
  40.6 0.0 all-to-all-done.after_ref.dec_ref
  40.6 0.1 shard_map.112
  40.7 0.0 copy-start.1
  40.7 0.0 copy-start.2
  40.7 0.0 copy-start.4
  40.8 0.0 copy-start.5
  40.8 23.3 %all_to_all.30 = bf16[4,1024,256]{2,1,0:T(8,128)(2,1)S(1)} all-to-all(bf16[4,1024,256]{2,1,0:T(8,128)(2,1)S(1)} %shard_map.112), channel_id=1, replica_groups=mesh['z'=16,'y'=4,'x'=4,'core'=2] {'y'}, dimensions={0} | all-to-all | bytes 4194304 | tf_op jit(solution)/shard_map/all_to_all | solution.py:253
  64.0 0.0 copy-done.1
  64.0 0.0 copy-done.2
  64.0 0.0 copy-done.4
  64.0 0.0 copy-done.5
  64.0 0.0 copy-start
  64.1 1.1 shard_map.113
  65.2 9.3 %all_to_all.31.feat_ref = bf16[4,256,256]{2,1,0:T(8,128)(2,1)S(1)} all-to-all(bf16[4,256,256]{2,1,0:T(8,128)(2,1)S(1)} %get-tuple-element.11), channel_id=1, replica_groups=mesh['z'=16,'y'=4,'x'=4,'core'=2] {'y'}, dimensions={0} | all-to-all | bytes 1048576 | tf_op jit(solution)/shard_map/all_to_all | solution.py:253
  74.5 0.0 copy-done
  74.5 0.0 copy-start.3
  74.5 0.8 shard_map.114
  75.3 26.4 %all_to_all.32.part_ref = bf16[16,64,256]{2,1,0:T(8,128)(2,1)S(1)} all-to-all(bf16[16,64,256]{2,1,0:T(8,128)(2,1)S(1)} %bitcast.11), channel_id=1, replica_groups={{256,288,320,352,384,416,448,480,0,32,64,96,128,160,192,224},{257,289,3..., dimensions={0} | all-to-all | bytes 1048576 | tf_op jit(solution)/shard_map/all_to_all | solution.py:257
  101.7 0.0 copy-done.3
  101.7 0.4 shard_map.115
  102.1 21.7 %all_to_all.33.in_ref = bf16[16,80,128]{2,1,0:T(8,128)(2,1)S(1)} all-to-all(bf16[16,80,128]{2,1,0:T(8,128)(2,1)S(1)} %shard_map.115), channel_id=1, replica_groups={{256,288,320,352,384,416,448,480,0,32,64,96,128,160,192,224},{257,289,3..., dimensions={0} | all-to-all | bytes 655360 | tf_op jit(solution)/shard_map/all_to_all | solution.py:257
  123.8 0.2 shard_map.116
  124.0 19.8 %all_to_all.34.in_ref = bf16[16,32,1152]{2,1,0:T(8,128)(2,1)S(1)} all-to-all(bf16[16,32,1152]{2,1,0:T(8,128)(2,1)S(1)} %shard_map.116), channel_id=1, replica_groups=mesh['z'=16,'y'=4,'x'=4,'core'=2] {'y','x'}, dimensions={0} | all-to-all | bytes 2359296 | tf_op jit(solution)/shard_map/all_to_all | solution.py:253
  143.8 0.5 shard_map.117.rows_ref
  144.3 10.0 %collective-permute-start = (bf16[128,4096]{1,0:T(8,128)(2,1)S(1)}, bf16[128,4096]{1,0:T(8,128)(2,1)S(1)}, u32[]{:S(2)}, u32[]{:S(2)}) collective-permute-start(bf16[128,4096]{1,0:T(8,128)(2,1)S(1)} %shard_map.117.rows_ref), channel_id=1, source_target_pairs={{0,1},{1,0},{2,3},{3,2},{4,5},{5,4},{6,7},{7,6},{8,9},{9,8},{10,11... | collective-permute-start | bytes 3145736 | tf_op jit(solution)/shard_map/ppermute | solution.py:321
  154.4 1.1 shard_map.118
  155.4 1.2 collective-permute-done.rows_ref
  156.6 1.5 shard_map.119
Async XLA Ops:
  2.9 5.0 %copy-start.6 = (bf16[64,256]{1,0:T(8,128)(2,1)S(1)}, bf16[64,256]{1,0:T(8,128)(2,1)}, u32[]{:S(2)}) copy-start(bf16[64,256]{1,0:T(8,128)(2,1)} %param.8) | copy-start | bytes 98308
  2.9 5.0 %copy-start.7 = (f32[64]{0:T(128)S(1)}, f32[64]{0:T(128)}, u32[]{:S(2)}) copy-start(f32[64]{0:T(128)} %param.9) | copy-start | bytes 772
  2.9 37.6 %all-to-all-start = ((bf16[4,256,1024]{2,1,0:T(8,128)(2,1)}), bf16[4,256,1024]{2,1,0:T(8,128)(2,1)S(1)}, u32[]{:S(2)}, u32[]{:S(2)}) async-start(bf16[4,256,1024]{2,1,0:T(8,128)(2,1)} %shard_map.111), calls=%async_computation | async-start | bytes 4194304 | tf_op jit(solution)/shard_map/all_to_all | solution.py:253
  40.7 23.3 %copy-start.1 = (bf16[4096,256]{1,0:T(8,128)(2,1)S(1)}, bf16[4096,256]{1,0:T(8,128)(2,1)}, u32[]{:S(2)}) copy-start(bf16[4096,256]{1,0:T(8,128)(2,1)} %enc_ref.1) | copy-start | bytes 6291460
  40.7 23.3 %copy-start.2 = (s32[64,8]{0,1:T(8,128)S(1)}, s32[64,8]{0,1:T(8,128)}, u32[]{:S(2)}) copy-start(s32[64,8]{0,1:T(8,128)} %param.14) | copy-start | bytes 6148
  40.7 23.3 %copy-start.4 = (f32[256]{0:T(256)S(1)}, f32[256]{0:T(256)}, u32[]{:S(2)}) copy-start(f32[256]{0:T(256)} %param.11) | copy-start | bytes 3076
  40.8 23.3 %copy-start.5 = (s32[1,256]{1,0:T(1,128)S(1)}, s32[1,256]{1,0:T(1,128)}, u32[]{:S(2)}) copy-start(s32[1,256]{1,0:T(1,128)} %dead_ref.1) | copy-start | bytes 3076
  64.0 10.4 %copy-start = (bf16[256,4096]{1,0:T(8,128)(2,1)S(1)}, bf16[256,4096]{1,0:T(8,128)(2,1)}, u32[]{:S(2)}) copy-start(bf16[256,4096]{1,0:T(8,128)(2,1)} %own_ref.1) | copy-start | bytes 6291460
  74.5 27.2 %copy-start.3 = (s32[64,1,32]{0,2,1:T(8,128)S(1)}, s32[64,1,32]{0,2,1:T(8,128)}, u32[]{:S(2)}) copy-start(s32[64,1,32]{0,2,1:T(8,128)} %param.15) | copy-start | bytes 24580
  144.3 12.3 %collective-permute-start = (bf16[128,4096]{1,0:T(8,128)(2,1)S(1)}, bf16[128,4096]{1,0:T(8,128)(2,1)S(1)}, u32[]{:S(2)}, u32[]{:S(2)}) collective-permute-start(bf16[128,4096]{1,0:T(8,128)(2,1)S(1)} %shard_map.117.rows_ref), channel_id=1, source_target_pairs={{0,1},{1,0},{2,3},{3,2},{4,5},{5,4},{6,7},{7,6},{8,9},{9,8},{10,11... | collective-permute-start | bytes 3145736 | tf_op jit(solution)/shard_map/ppermute | solution.py:321
